TPU v7x, 32 devices: a whole 2x2x4 slice. The times are simulated.
32 devices in a mesh: dp: 8 (over z, x), mp: 4 (over y, core).
Axes of the slice: x: 2, y: 2, z: 4, core: 2. Of those that a mesh axis runs over, the one named last changes fastest.
Arguments:
- inputs: bfloat16 [16384, 768], P(('dp', 'mp')), may hold values from -6 to 6
- cotangent: bfloat16 [16384, 768], P(('dp', 'mp')), may hold values from -6 to 6
- ln1_gain: float32 [768], replicated, may hold values from 0.1 to 1.9
- ln1_bias: float32 [768], replicated, may hold values from -3 to 3
- w_qkv: bfloat16 [3, 768, 768], P(None, None, 'mp'), may hold values from -0.21875 to 0.21875
- qv_bias: float32 [2, 768], P(None, 'mp'), may hold values from -3 to 3
- w_out: bfloat16 [768, 768], P('mp'), may hold values from -1.25 to 1.25
- out_bias: float32 [768], replicated, may hold values from -3 to 3
- ln2_gain: float32 [768], replicated, may hold values from 0.1 to 1.9
- ln2_bias: float32 [768], replicated, may hold values from -3 to 3
- w_fc: bfloat16 [768, 3072], P(None, 'mp'), may hold values from -0.21875 to 0.21875
- fc_bias: float32 [3072], P('mp'), may hold values from -3 to 3
- w_proj: bfloat16 [3072, 768], P('mp'), may hold values from -0.3125 to 0.3125
- proj_bias: float32 [768], replicated, may hold values from -3 to 3
- doc_lengths: int32 [16, 4], P('dp'), may hold values from 0 to 1024, as said below
Outputs:
- layer_out: bfloat16 [16384, 768], P(('dp', 'mp'))
- input_grad: bfloat16 [16384, 768], P(('dp', 'mp'))
- ln1_gain_grad: float32 [768], replicated
- ln1_bias_grad: float32 [768], replicated
- qkv_grad: float32 [3, 768, 768], P(None, None, 'mp')
- qv_bias_grad: float32 [2, 768], P(None, 'mp')
- out_weight_grad: float32 [768, 768], P('mp')
- out_bias_grad: float32 [768], replicated
- ln2_gain_grad: float32 [768], replicated
- ln2_bias_grad: float32 [768], replicated
- fc_weight_grad: float32 [768, 3072], P(None, 'mp')
- fc_bias_grad: float32 [3072], P('mp')
- proj_weight_grad: float32 [3072, 768], P('mp')
- proj_bias_grad: float32 [768], replicated
Inputs may be any that keep to these rules, and one draw needn't show every extreme that they name: `doc_lengths`: each row lists the lengths of its packed documents in order, each 1 or more, then zeros; a row's lengths add up to between 973 and 1024, and positions past the sum are padding. Some row holds a single document of all 1024 positions.
All inputs are finite; a program needn't handle non-finite values.
Results may differ from a plain program's by a relative error of at most 0.017.
Values may be sent and summed in bfloat16 or wider, within the bound.
A program may use at most 128 MiB of HBM per device.

v0:
```python
import math

import jax
import jax.numpy as jnp
from jax import lax
from jax.sharding import PartitionSpec as P

HD = 64


branch_scale = 12 ** (-0.5)


def normalize(values, gain, shift):
    average = jnp.mean(values, axis=-1, keepdims=True)
    centred = values - average
    spread = jnp.mean(centred * centred, axis=-1, keepdims=True)
    return centred * lax.rsqrt(spread + 1e-05) * gain + shift


def gelu_tanh(values):
    return jax.nn.gelu(values, approximate=True)


def segment_ids(lengths, length):
    ends = jnp.cumsum(lengths, axis=1)
    places = jnp.arange(length, dtype=jnp.int32)
    return jnp.sum((places[None, :, None] >= ends[:, None, :]).astype(jnp.int32), axis=-1)


def visible_keys(segments, docs):
    places = jnp.arange(segments.shape[0], dtype=jnp.int32)
    same = segments[:, None] == segments[None, :]
    causal = places[None, :] <= places[:, None]
    real = segments[None, :] < docs
    return same & causal & real | (places[:, None] == places[None, :])


def masked_scores(query_row, key_row, segment_row, docs, factor):
    scores = (
        jnp.einsum("qhd,khd->hqk", query_row, key_row, preferred_element_type=jnp.float32) * factor
    )
    return jnp.where(visible_keys(segment_row, docs)[None], scores, -1e30)


def attend_forward(queries, key_rows, value_rows, segments, docs, head_size):
    factor = 1.0 / math.sqrt(head_size)
    shape4 = (segments.shape[0], segments.shape[1], queries.shape[1] // head_size, head_size)

    def one_row(row):
        query_row, key_row, value_row, segment_row = row
        scores = masked_scores(query_row, key_row, segment_row, docs, factor)
        peak = jnp.max(scores, axis=-1, keepdims=True)
        exponent = jnp.exp(scores - peak)
        total = jnp.sum(exponent, axis=-1, keepdims=True)
        probs = exponent / total
        mixed = jnp.einsum(
            "hqk,khd->qhd",
            probs.astype(jnp.bfloat16),
            value_row,
            preferred_element_type=jnp.float32,
        )
        return (mixed.astype(jnp.bfloat16), peak[..., 0] + jnp.log(total[..., 0]))

    mixed, log_total = lax.map(
        one_row,
        (queries.reshape(shape4), key_rows.reshape(shape4), value_rows.reshape(shape4), segments),
    )
    return (mixed.reshape(queries.shape), log_total)


def attend_backward(
    queries, key_rows, value_rows, mixed_grad, log_total, segments, docs, head_size
):
    factor = 1.0 / math.sqrt(head_size)
    shape4 = (segments.shape[0], segments.shape[1], queries.shape[1] // head_size, head_size)

    def one_row(row):
        query_row, key_row, value_row, grad_row, total_row, segment_row = row
        scores = masked_scores(query_row, key_row, segment_row, docs, factor)
        probs = jnp.exp(scores - total_row[..., None])
        prob_grad = jnp.einsum(
            "qhd,khd->hqk", grad_row, value_row, preferred_element_type=jnp.float32
        )
        inner = jnp.sum(probs * prob_grad, axis=-1, keepdims=True)
        score_grad = (probs * (prob_grad - inner)).astype(jnp.bfloat16)
        query_grad = (
            jnp.einsum("hqk,khd->qhd", score_grad, key_row, preferred_element_type=jnp.float32)
            * factor
        ).astype(jnp.bfloat16)
        key_grad = (
            jnp.einsum("hqk,qhd->khd", score_grad, query_row, preferred_element_type=jnp.float32)
            * factor
        ).astype(jnp.bfloat16)
        value_grad = jnp.einsum(
            "hqk,qhd->khd", probs.astype(jnp.bfloat16), grad_row, preferred_element_type=jnp.float32
        ).astype(jnp.bfloat16)
        return (query_grad, key_grad, value_grad)

    query_grad, key_grad, value_grad = lax.map(
        one_row,
        (
            queries.reshape(shape4),
            key_rows.reshape(shape4),
            value_rows.reshape(shape4),
            mixed_grad.reshape(shape4),
            log_total,
            segments,
        ),
    )
    return (
        query_grad.reshape(queries.shape),
        key_grad.reshape(queries.shape),
        value_grad.reshape(queries.shape),
    )


def shards(
    inputs,
    cotangent,
    ln1_gain,
    ln1_bias,
    w_qkv,
    qv_bias,
    w_out,
    out_bias,
    ln2_gain,
    ln2_bias,
    w_fc,
    fc_bias,
    w_proj,
    proj_bias,
    doc_lengths,
):
    docs = doc_lengths.shape[1]
    shard_rows = inputs.shape[0]
    all_rows = shard_rows * lax.axis_size("mp")
    seq_len = all_rows // doc_lengths.shape[0]
    segments = segment_ids(doc_lengths, seq_len)
    state = inputs.astype(jnp.float32)
    out_grad = cotangent.astype(jnp.float32)

    def front(source):
        normed1 = normalize(source, ln1_gain, ln1_bias).astype(jnp.bfloat16)
        normed1_all = lax.all_gather(normed1, "mp", axis=0, tiled=True)
        projected = jnp.einsum(
            "td,cde->cte", normed1_all, w_qkv, preferred_element_type=jnp.float32
        )
        queries = (projected[0] + qv_bias[0]).astype(jnp.bfloat16)
        key_rows = projected[1].astype(jnp.bfloat16)
        value_rows = (projected[2] + qv_bias[1]).astype(jnp.bfloat16)
        mixed, log_total = attend_forward(queries, key_rows, value_rows, segments, docs, HD)
        attn = lax.psum_scatter(
            jnp.dot(mixed, w_out, preferred_element_type=jnp.float32).astype(jnp.bfloat16),
            "mp",
            scatter_dimension=0,
            tiled=True,
        ).astype(jnp.float32)
        hidden = source + branch_scale * (attn + out_bias)
        return (normed1_all, queries, key_rows, value_rows, mixed, log_total, hidden)

    def mlp_front(hidden):
        normed2 = normalize(hidden, ln2_gain, ln2_bias).astype(jnp.bfloat16)
        normed2_all = lax.all_gather(normed2, "mp", axis=0, tiled=True)
        pre_act = jnp.dot(normed2_all, w_fc, preferred_element_type=jnp.float32) + fc_bias
        activ = gelu_tanh(pre_act).astype(jnp.bfloat16)
        return (normed2_all, pre_act, activ)

    normed1_all, queries, key_rows, value_rows, mixed, log_total, hidden = front(state)
    normed2_all, pre_act, activ = mlp_front(hidden)
    mlp = lax.psum_scatter(
        jnp.dot(activ, w_proj, preferred_element_type=jnp.float32).astype(jnp.bfloat16),
        "mp",
        scatter_dimension=0,
        tiled=True,
    ).astype(jnp.float32)
    layer_out = (hidden + branch_scale * (mlp + proj_bias)).astype(jnp.bfloat16)
    anchor = lax.optimization_barrier((state, out_grad))[0]
    normed1_all, queries, key_rows, value_rows, mixed, log_total, hidden = front(anchor)
    normed2_all, pre_act, activ = mlp_front(hidden)
    proj_bias_grad = branch_scale * jnp.sum(out_grad, axis=0)
    mlp_grad = (branch_scale * out_grad).astype(jnp.bfloat16)
    mlp_grad_all = lax.all_gather(mlp_grad, "mp", axis=0, tiled=True)
    proj_weight_grad = jnp.einsum(
        "tf,td->fd", activ, mlp_grad_all, preferred_element_type=jnp.float32
    )
    activ_grad = jnp.einsum("td,fd->tf", mlp_grad_all, w_proj, preferred_element_type=jnp.float32)
    gelu_back = jax.vjp(gelu_tanh, pre_act)[1]
    pre_grad = gelu_back(activ_grad)[0]
    fc_bias_grad = jnp.sum(pre_grad, axis=0)
    pre_low = pre_grad.astype(jnp.bfloat16)
    fc_weight_grad = jnp.einsum(
        "td,tf->df", normed2_all, pre_low, preferred_element_type=jnp.float32
    )
    norm2_grad = lax.psum_scatter(
        jnp.einsum("tf,df->td", pre_low, w_fc, preferred_element_type=jnp.float32).astype(
            jnp.bfloat16
        ),
        "mp",
        scatter_dimension=0,
        tiled=True,
    ).astype(jnp.float32)
    norm2_back = jax.vjp(normalize, hidden, ln2_gain, ln2_bias)[1]
    hidden_part, ln2_gain_grad, ln2_bias_grad = norm2_back(norm2_grad)
    hidden_grad = out_grad + hidden_part
    out_bias_grad = branch_scale * jnp.sum(hidden_grad, axis=0)
    attn_grad = (branch_scale * hidden_grad).astype(jnp.bfloat16)
    attn_grad_all = lax.all_gather(attn_grad, "mp", axis=0, tiled=True)
    out_weight_grad = jnp.einsum(
        "te,td->ed", mixed, attn_grad_all, preferred_element_type=jnp.float32
    )
    mixed_grad = jnp.einsum(
        "td,ed->te", attn_grad_all, w_out, preferred_element_type=jnp.float32
    ).astype(jnp.bfloat16)
    query_grad, key_grad, value_grad = attend_backward(
        queries, key_rows, value_rows, mixed_grad, log_total, segments, docs, HD
    )
    qv_bias_grad = jnp.stack(
        [
            jnp.sum(query_grad.astype(jnp.float32), axis=0),
            jnp.sum(value_grad.astype(jnp.float32), axis=0),
        ]
    )
    stacked_grad = jnp.stack([query_grad, key_grad, value_grad])
    qkv_grad = jnp.einsum(
        "td,cte->cde", normed1_all, stacked_grad, preferred_element_type=jnp.float32
    )
    norm1_grad = lax.psum_scatter(
        jnp.einsum("cte,cde->td", stacked_grad, w_qkv, preferred_element_type=jnp.float32).astype(
            jnp.bfloat16
        ),
        "mp",
        scatter_dimension=0,
        tiled=True,
    ).astype(jnp.float32)
    norm1_back = jax.vjp(normalize, state, ln1_gain, ln1_bias)[1]
    state_part, ln1_gain_grad, ln1_bias_grad = norm1_back(norm1_grad)
    input_grad = (hidden_grad + state_part).astype(jnp.bfloat16)
    qkv_grad, qv_bias_grad, out_weight_grad, fc_weight_grad, fc_bias_grad, proj_weight_grad = (
        lax.psum(
            (
                qkv_grad,
                qv_bias_grad,
                out_weight_grad,
                fc_weight_grad,
                fc_bias_grad,
                proj_weight_grad,
            ),
            "dp",
        )
    )
    ln1_gain_grad, ln1_bias_grad, out_bias_grad, ln2_gain_grad, ln2_bias_grad, proj_bias_grad = (
        lax.psum(
            (
                ln1_gain_grad,
                ln1_bias_grad,
                out_bias_grad,
                ln2_gain_grad,
                ln2_bias_grad,
                proj_bias_grad,
            ),
            ("dp", "mp"),
        )
    )
    return (
        layer_out,
        input_grad,
        ln1_gain_grad,
        ln1_bias_grad,
        qkv_grad,
        qv_bias_grad,
        out_weight_grad,
        out_bias_grad,
        ln2_gain_grad,
        ln2_bias_grad,
        fc_weight_grad,
        fc_bias_grad,
        proj_weight_grad,
        proj_bias_grad,
    )


def solution(mesh):
    in_specs = (
        P(("dp", "mp"), None),
        P(("dp", "mp"), None),
        P(),
        P(),
        P(None, None, "mp"),
        P(None, "mp"),
        P("mp", None),
        P(),
        P(),
        P(),
        P(None, "mp"),
        P("mp"),
        P("mp", None),
        P(),
        P("dp", None),
    )
    out_specs = (
        P(("dp", "mp"), None),
        P(("dp", "mp"), None),
        P(),
        P(),
        P(None, None, "mp"),
        P(None, "mp"),
        P("mp", None),
        P(),
        P(),
        P(),
        P(None, "mp"),
        P("mp"),
        P("mp", None),
        P(),
    )
    return jax.shard_map(shards, mesh=mesh, in_specs=in_specs, out_specs=out_specs, check_vma=False)
```

profile of v0, /device:TPU:0, one launch (start us, length us, event | category | flops | bytes accessed | tf_op | source)
XLA Modules:
  0.0 907.3 jit_solution(13359767046625783920)
XLA Ops:
  10.9 30.8 %all-gather.13.cloned.1.call-done = bf16[2048,768]{1,0:T(8,128)(2,1)} async-done(((bf16[512,768]{1,0:T(8,128)(2,1)}), bf16[2048,768]{1,0:T(8,128)(2,1)}) %all-gather.13.cloned.1.call-update) | async-done | bytes 3145744 | tf_op jit(solution)/shard_map/all_gather | solution.py:145
  62.9 49.5 %while.37 = (s32[]{:T(128)}, bf16[2,1024,3,64]{1,3,2,0:T(8,128)(2,1)}, f32[2,3,1024]{2,1,0:T(4,128)}, bf16[2,1024,3,64]{1,3,2,0:T(8,128)(2,1)}, s32[2,1024]{1,0:...) while((s32[]{:T(128)}, ...), condition=%wide.region_17.18_spmd, body=%wide.region_14.17_spmd.sunk | while | flops 849541120 | bytes 53285104 | solution.py:65
  71.8 7.4 fusion.236
  96.4 7.4 fusion.236
  118.3 38.1 %reduce-scatter.10.cloned.1.call-done = bf16[512,768]{1,0:T(8,128)(2,1)} async-done(((bf16[2048,768]{1,0:T(8,128)(2,1)}), bf16[512,768]{1,0:T(8,128)(2,1)}) %reduce-scatter.10.cloned.1.call-update) | async-done | bytes 786448 | tf_op jit(solution)/shard_map/reduce_scatter | solution.py:153
  161.3 27.5 %all-gather.15.cloned.1.call-done = bf16[2048,768]{1,0:T(8,128)(2,1)} async-done(((bf16[512,768]{1,0:T(8,128)(2,1)}), bf16[2048,768]{1,0:T(8,128)(2,1)}) %all-gather.15.cloned.1.call-update) | async-done | bytes 3145744 | tf_op jit(solution)/shard_map/all_gather | solution.py:164
  196.0 23.5 %all-gather.11.cloned.1.call-done = bf16[2048,768]{1,0:T(8,128)(2,1)} async-done(((bf16[512,768]{1,0:T(8,128)(2,1)}), bf16[2048,768]{1,0:T(8,128)(2,1)}) %all-gather.11.cloned.1.call-update) | async-done | bytes 3145744 | tf_op jit(solution)/shard_map/all_gather | solution.py:183
  219.5 9.9 %fusion.155 = (f32[768]{0:T(1024)}, bf16[2048,768]{1,0:T(8,128)(2,1)S(1)}) fusion(f32[2048,768]{1,0:T(8,128)} %fusion.172, f32[768]{0:T(1024)S(1)} %copy-done.61, bf16[2048,768]{1,0:T(8,128)(2,1)} %all-gather.11.cloned.1.call-done, bf16[768,768]{1,0:T(8,128)(2,1)} %param.33), kind=kOutput, calls=%fused_computation.223 | convolution fusion | flops 2450521344 | bytes 13768704 | tf_op jit(solution)/shard_map/td,fd->tf/dot_general | solution.py:187
  235.2 38.0 %reduce-scatter.12.cloned.1.call-done = bf16[512,768]{1,0:T(8,128)(2,1)} async-done(((bf16[2048,768]{1,0:T(8,128)(2,1)}), bf16[512,768]{1,0:T(8,128)(2,1)}) %reduce-scatter.12.cloned.1.call-update) | async-done | bytes 786448 | tf_op jit(solution)/shard_map/reduce_scatter | solution.py:195
  281.6 28.3 %all-gather.17.cloned.1.call-done = bf16[2048,768]{1,0:T(8,128)(2,1)} async-done(((bf16[512,768]{1,0:T(8,128)(2,1)}), bf16[2048,768]{1,0:T(8,128)(2,1)}) %all-gather.17.cloned.1.call-update) | async-done | bytes 3145744 | tf_op jit(solution)/shard_map/all_gather | solution.py:208
  318.7 53.5 %while.38 = (s32[]{:T(128)}, bf16[2,1024,3,64]{1,3,2,0:T(8,128)(2,1)}, bf16[2,1024,3,64]{1,3,2,0:T(8,128)(2,1)}, bf16[2,1024,3,64]{1,3,2,0:T(8,128)(2,1)}, bf16[...) while((s32[]{:T(128)}, ...), condition=%wide.region_26.27_spmd, body=%wide.region_24.26_spmd.sunk | while | flops 2067724288 | bytes 124632392 | solution.py:100
  327.0 7.2 multiply_reduce_fusion.6
  393.3 36.8 %reduce-scatter.14.cloned.1.call-done = bf16[512,768]{1,0:T(8,128)(2,1)} async-done(((bf16[2048,768]{1,0:T(8,128)(2,1)}), bf16[512,768]{1,0:T(8,128)(2,1)}) %reduce-scatter.14.cloned.1.call-update) | async-done | bytes 786448 | tf_op jit(solution)/shard_map/reduce_scatter | solution.py:228
  434.5 28.6 %all-gather.7.cloned.1.call-done = bf16[2048,768]{1,0:T(8,128)(2,1)} async-done(((bf16[512,768]{1,0:T(8,128)(2,1)}), bf16[2048,768]{1,0:T(8,128)(2,1)}) %all-gather.7.cloned.1.call-update) | async-done | bytes 3145744 | tf_op jit(solution)/shard_map/all_gather | solution.py:145
  487.2 38.4 %while.36 = (s32[]{:T(128)}, bf16[2,1024,3,64]{1,3,2,0:T(8,128)(2,1)}, bf16[2,1024,3,64]{1,3,2,0:T(8,128)(2,1)}, s32[2,1024]{1,0:T(2,128)S(1)}, bf16[2,1024,3,64...) while((s32[]{:T(128)}, bf16[2,1024,3,64]{1,3,2,0:T(8,128)(2,1)}, ...), condition=%wide.region_7.8_spmd, body=%wide.region_4.7_spmd.sunk | while | flops 830670848 | bytes 28876888 | solution.py:65
  489.6 10.4 %fusion.231 = (f32[3,1024]{1,0:T(4,128)S(1)}, f32[3,1024,1024]{1,2,0:T(8,128)}) fusion(pred[1024,1024]{0,1:T(8,128)(4,1)S(1)} %fusion.230, bf16[2,1024,3,64]{1,3,2,0:T(8,128)(2,1)} %get-tuple-element.558, s32[]{:T(128)S(6)} %copy.131, bf16[2,1024,3,64]{1,3,2,0:T(8,128)(2,1)} %get-tuple-element.557), kind=kOutput, calls=%fused_computation.226.clone.1 | convolution fusion | flops 415237120 | bytes 14431232 | tf_op jit(solution)/shard_map/while/body/eval_jaxpr/sub | solution.py:54
  508.6 10.4 %fusion.231 = (f32[3,1024]{1,0:T(4,128)S(1)}, f32[3,1024,1024]{1,2,0:T(8,128)}) fusion(pred[1024,1024]{0,1:T(8,128)(4,1)S(1)} %fusion.230, bf16[2,1024,3,64]{1,3,2,0:T(8,128)(2,1)} %get-tuple-element.558, s32[]{:T(128)S(6)} %copy.131, bf16[2,1024,3,64]{1,3,2,0:T(8,128)(2,1)} %get-tuple-element.557), kind=kOutput, calls=%fused_computation.226.clone.1 | convolution fusion | flops 415237120 | bytes 14431232 | tf_op jit(solution)/shard_map/while/body/eval_jaxpr/sub | solution.py:54
  530.6 38.1 %reduce-scatter.6.cloned.1.call-done = bf16[512,768]{1,0:T(8,128)(2,1)} async-done(((bf16[2048,768]{1,0:T(8,128)(2,1)}), bf16[512,768]{1,0:T(8,128)(2,1)}) %reduce-scatter.6.cloned.1.call-update) | async-done | bytes 786448 | tf_op jit(solution)/shard_map/reduce_scatter | solution.py:153
  575.0 28.6 %all-gather.9.cloned.1.call-done = bf16[2048,768]{1,0:T(8,128)(2,1)} async-done(((bf16[512,768]{1,0:T(8,128)(2,1)}), bf16[2048,768]{1,0:T(8,128)(2,1)}) %all-gather.9.cloned.1.call-update) | async-done | bytes 3145744 | tf_op jit(solution)/shard_map/all_gather | solution.py:164
  603.6 9.1 %convolution_convert_fusion.1 = bf16[2048,768]{1,0:T(8,128)(2,1)} fusion(bf16[768,768]{1,0:T(8,128)(2,1)} %param.33, bf16[2048,768]{1,0:T(8,128)(2,1)} %all-gather.9.cloned.1.call-done, bf16[768,768]{1,0:T(8,128)(2,1)S(1)} %copy-done, f32[768]{0:T(1024)S(1)} %copy-done.62), kind=kOutput, calls=%fused_computation.132 | convolution fusion | flops 4849139712 | bytes 8653824 | tf_op jit(solution)/shard_map/dot_general | solution.py:172
  619.9 8.6 fusion.123
  643.9 22.5 %all-reduce.1 = (f32[2,192]{1,0:T(2,128)}, f32[768]{0:T(1024)}) all-reduce(f32[2,192]{1,0:T(2,128)} %pad_maximum_fusion, f32[768]{0:T(1024)} %get-tuple-element.292), channel_id=1, replica_groups=mesh['dp'=8,'mp'=4] {'dp'}, use_global_device_ids=true, to_apply=%region_37.38 | all-reduce | flops 1152 | bytes 9216 | tf_op jit(solution)/shard_map/psum | solution.py:240
  666.4 42.6 %all-reduce = (f32[768]{0:T(1024)}, f32[768]{0:T(1024)}, f32[768]{0:T(1024)}, f32[768]{0:T(1024)}, f32[768]{0:T(1024)}, /*index=5*/f32[768]{0:T(1024)}) all-reduce(f32[768]{0:T(1024)} %get-tuple-element.217, f32[768]{0:T(1024)} %get-tuple-element.224, f32[768]{0:T(1024)} %broadcast_multiply_fusion.1, ...), channel_id=1, replica_groups=mesh['dp'=8,'mp'=4] {'dp','mp'}, use_global_device_ids=true, to_apply=%region_31.32 | all-reduce | flops 4608 | bytes 36864 | tf_op jit(solution)/shard_map/psum | solution.py:253
  713.8 179.9 %all-reduce.5.cloned.1.call-done = (f32[3,768,192]{1,2,0:T(8,128)}, f32[192,768]{1,0:T(8,128)}, f32[768,768]{1,0:T(8,128)}, f32[768,768]{1,0:T(8,128)}) async-done(((f32[3,768,192]{1,2,0:T(8,128)}, f32[192,768]{1,0:T(8,128)}, f32[768,768]{1,0:T(8,128)}, f32[768,768]{1,0:T(8,128)}), (f32[3,768,192]{1,2,0:T(8,128)}, f32[192,768]{1,0:T(8,128)}, f32[768,768]{1,0:T(8,128)}, ...) | async-done | bytes 7077904 | tf_op jit(solution)/shard_map/psum | solution.py:240
  (302 shorter events, 257.6 us)
Async XLA Ops:
  7.2 181.7 %copy-start = (bf16[768,768]{1,0:T(8,128)(2,1)S(1)}, bf16[768,768]{1,0:T(8,128)(2,1)}, u32[]{:S(2)}) copy-start(bf16[768,768]{1,0:T(8,128)(2,1)} %param.31) | copy-start | bytes 3538948
  7.2 34.5 %all-gather.13.cloned.1.call-start = ((), (), s32[]{:S(2)}) async-start(), calls=%async_computation.10 | async-start | bytes 3932160 | tf_op jit(solution)/shard_map/all_gather | solution.py:145
  10.3 146.0 %reduce-scatter.10.cloned.1.call-start = ((), (), s32[]{:S(2)}) async-start(), calls=%async_computation.11 | async-start | bytes 3932160 | tf_op jit(solution)/shard_map/reduce_scatter | solution.py:153
  10.7 47.2 %copy-start.50 = (f32[3,64]{1,0:T(4,128)}, f32[3,64]{1,0:T(4,128)S(1)}, u32[]{:S(2)}) copy-start(f32[3,64]{1,0:T(4,128)S(1)} %add.230) | copy-start | bytes 2308
  10.8 47.1 %copy-start.49 = (f32[3,64]{1,0:T(4,128)}, f32[3,64]{1,0:T(4,128)S(1)}, u32[]{:S(2)}) copy-start(f32[3,64]{1,0:T(4,128)S(1)} %add.227) | copy-start | bytes 2308
  118.2 40.8 %copy-start.40 = (f32[768]{0:T(1024)S(1)}, f32[768]{0:T(1024)}, u32[]{:S(2)}) copy-start(f32[768]{0:T(1024)} %param.29) | copy-start | bytes 9220
  118.2 70.6 %all-gather.15.cloned.1.call-start = ((), (), s32[]{:S(2)}) async-start(), calls=%async_computation.12 | async-start | bytes 3932160 | tf_op jit(solution)/shard_map/all_gather | solution.py:164
  160.2 59.3 %all-gather.11.cloned.1.call-start = ((), (), s32[]{:S(2)}) async-start(), calls=%async_computation.9 | async-start | bytes 3932160 | tf_op jit(solution)/shard_map/all_gather | solution.py:183
  161.3 58.2 %copy-start.61 = (f32[768]{0:T(1024)S(1)}, f32[768]{0:T(1024)}, u32[]{:S(2)}) copy-start(f32[768]{0:T(1024)} %param.32) | copy-start | bytes 9220
  161.3 111.9 %reduce-scatter.12.cloned.1.call-start = ((), (), s32[]{:S(2)}) async-start(), calls=%async_computation.13 | async-start | bytes 3932160 | tf_op jit(solution)/shard_map/reduce_scatter | solution.py:195
  235.1 74.8 %all-gather.17.cloned.1.call-start = ((), (), s32[]{:S(2)}) async-start(), calls=%async_computation.14 | async-start | bytes 3932160 | tf_op jit(solution)/shard_map/all_gather | solution.py:208
  281.2 148.9 %reduce-scatter.14.cloned.1.call-start = ((), (), s32[]{:S(2)}) async-start(), calls=%async_computation.15 | async-start | bytes 3932160 | tf_op jit(solution)/shard_map/reduce_scatter | solution.py:228
  392.0 41.2 %copy-start.52 = (f32[768]{0:T(1024)S(1)}, f32[768]{0:T(1024)}, u32[]{:S(2)}) copy-start(f32[768]{0:T(1024)} %param.24) | copy-start | bytes 9220
  392.0 71.1 %copy-start.60 = (bf16[3,768,192]{1,2,0:T(8,128)(2,1)S(1)}, bf16[3,768,192]{1,2,0:T(8,128)(2,1)}, u32[]{:S(2)}) copy-start(bf16[3,768,192]{1,2,0:T(8,128)(2,1)} %param.25) | copy-start | bytes 2654212
  392.0 71.1 %all-gather.7.cloned.1.call-start = ((), (), s32[]{:S(2)}) async-start(), calls=%async_computation.5 | async-start | bytes 3932160 | tf_op jit(solution)/shard_map/all_gather | solution.py:145
  434.4 134.3 %reduce-scatter.6.cloned.1.call-start = ((), (), s32[]{:S(2)}) async-start(), calls=%async_computation.6 | async-start | bytes 3932160 | tf_op jit(solution)/shard_map/reduce_scatter | solution.py:153
  530.5 39.8 %copy-start.46 = (f32[512]{0:T(512)S(1)}, f32[512]{0:T(512)}, u32[]{:S(2)}) copy-start(f32[512]{0:T(512)} %get-tuple-element.311) | copy-start | bytes 6148
  530.5 43.0 %copy-start.41 = (f32[768]{0:T(1024)S(1)}, f32[768]{0:T(1024)}, u32[]{:S(2)}) copy-start(f32[768]{0:T(1024)} %param.29) | copy-start | bytes 9220
  530.6 43.0 %copy-start.54 = (f32[768]{0:T(1024)S(1)}, f32[768]{0:T(1024)}, u32[]{:S(2)}) copy-start(f32[768]{0:T(1024)} %param.30) | copy-start | bytes 9220
  530.6 73.1 %all-gather.9.cloned.1.call-start = ((), (), s32[]{:S(2)}) async-start(), calls=%async_computation.7 | async-start | bytes 3932160 | tf_op jit(solution)/shard_map/all_gather | solution.py:164
  575.0 135.3 %reduce-scatter.8.cloned.1.call-start = ((), (), s32[]{:S(2)}) async-start(), calls=%async_computation.8 | async-start | bytes 3932160 | tf_op jit(solution)/shard_map/reduce_scatter | solution.py:171
  612.7 281.0 %all-reduce.5.cloned.1.call-start = ((), (), s32[]{:S(2)}) async-start(), calls=%async_computation.16 | async-start | bytes 14155776 | tf_op jit(solution)/shard_map/psum | solution.py:240
  633.4 76.8 %copy-start.6 = (f32[512,768]{1,0:T(8,128)S(1)}, f32[512,768]{1,0:T(8,128)}, u32[]{:S(2)}) copy-start(f32[512,768]{1,0:T(8,128)} %copy-done.5) | copy-start | bytes 4718596
  633.4 76.8 %copy-start.44 = (f32[512]{0:T(512)S(1)}, f32[512]{0:T(512)}, u32[]{:S(2)}) copy-start(f32[512]{0:T(512)} %copy-done.42) | copy-start | bytes 6148
  (64 other events, 636.7 us)
Sparse Core Ops, SparseCore 0:
  10.4 31.2 all-gather.12
  118.3 37.9 reduce-scatter.9
  160.3 28.5 all-gather.14
  190.9 28.5 all-gather.10
  235.2 37.9 reduce-scatter.11
  281.3 28.5 all-gather.16
  392.1 37.9 reduce-scatter.13
  434.5 28.5 all-gather.6
  530.7 37.9 reduce-scatter.5
  575.1 28.5 all-gather.8
  612.9 37.9 reduce-scatter.7
  656.9 236.7 all-reduce.4
where the time goes:
time: 911 us; the launch traced here: 907 us
  waiting for transfers between devices  498 us (55%)
  matrix products  165 us (18%)
  other arithmetic  87.4 us (10%)
  local copies, waits for them, and re-layouts  74.8 us (8%)
  blocking collectives  65.2 us (7%)
  between operations  14.9 us (2%)
    psum x1, waiting for transfers between devices, shards(): lax.psum((qkv_grad, qv_bias_grad, out_weight_grad, fc_weight_grad, fc_bia...  180 us
    reduce_scatter x2, waiting for transfers between devices, front(): lax.psum_scatter(jnp.dot(mixed, w_out, preferred_element_type=jnp.float32...  76.1 us
    all_gather x2, waiting for transfers between devices, front(): normed1_all = lax.all_gather(normed1, 'mp', axis=0, tiled=True)  59.5 us
    all_gather x2, waiting for transfers between devices, mlp_front(): normed2_all = lax.all_gather(normed2, 'mp', axis=0, tiled=True)  56.2 us
    psum x1, blocking collectives, shards(): lax.psum((ln1_gain_grad, ln1_bias_grad, out_bias_grad, ln2_gain_grad, ln2...  42.6 us
    reduce_scatter x1, waiting for transfers between devices, shards(): lax.psum_scatter(jnp.einsum('tf,df->td', pre_low, w_fc, preferred_element...  38 us
    reduce_scatter x1, waiting for transfers between devices, shards(): lax.psum_scatter(jnp.einsum('cte,cde->td', stacked_grad, w_qkv, preferred...  36.8 us
    all_gather x1, waiting for transfers between devices, shards(): attn_grad_all = lax.all_gather(attn_grad, 'mp', axis=0, tiled=True)  28.3 us
  transfers between devices with their start and end apart: 12, of which 11 were waited for; matrix products, arithmetic and copies ran while one was open for 5% of the time, Pallas kernels for 0%

commit v1 on v0

v1 whole, which is shorter than its diff:
```python
import functools
import math

import jax
import jax.numpy as jnp
from jax import lax
from jax.experimental import pallas as pl
from jax.experimental.pallas import tpu as pltpu
from jax.sharding import PartitionSpec as P

HD = 64
SCALE = 12 ** (-0.5)
MESH = pl.DeviceIdType.MESH
F32 = jnp.float32
BF16 = jnp.bfloat16
NN = (((1,), (0,)), ((), ()))
NT = (((1,), (1,)), ((), ()))
TN = (((0,), (0,)), ((), ()))
BLOCK = 256
CHUNKS = 6
LN1G, LN1B, OUTB, LN2G, LN2B, PROJB, FCB, QVB = range(8)


def dot(a, b, dims=NN):
    return lax.dot_general(a, b, dims, preferred_element_type=F32)


def rows_of(start, size, align=16):
    return pl.ds(pl.multiple_of(start, align), size)


def centre(values):
    average = jnp.mean(values, axis=-1, keepdims=True)
    centred = values - average
    spread = jnp.mean(centred * centred, axis=-1, keepdims=True)
    rate = lax.rsqrt(spread + 1e-05)
    return centred * rate, rate


def block_kernel(
    x_ref, cot_ref, g1, b1, wqkv_hbm, qvb, wout_hbm, ob, g2, b2, wfc_hbm, fcb, wproj_hbm, pb, docs,
    layer_out, input_grad, grads, small_out,
    wqkv, wout, wfc, wproj, qvb_o, fcb_o, n1, n2, mg, ag, qh, kh, vh, mxh, mgh, p0, p1, p2, p3,
    s0, s1, s2, s3, act_t, plo, hid, hg, send_a, send_b, r_attn, r_mlp, r_n2,
    g_own, g_oth, y_in, x_in, z_in, piece, lo, sm_a, sm_b, sm_c, sm_d, sm_rc, sm_ry, sm_rx, sm_rz,
    cs, cr, ws, wr, fs, fr, ls, ys, yr, xs, xr, zs, zr, gs, gr, es, er, ks,
):
    half, width = x_ref.shape
    rows = 2 * half
    shard = wout_hbm.shape[0]
    nh = shard // HD
    hidden = wproj_hbm.shape[0]
    nblk = rows // BLOCK
    dp, mp = lax.axis_index("dp"), lax.axis_index("mp")
    core, y = lax.rem(mp, 2), lax.div(mp, 2)
    xi = lax.rem(dp, 2)
    zi = lax.rem(lax.div(dp, 2), 4)
    base = dp - 2 * zi
    core_id = (dp, mp + 1 - 2 * core)
    y_id = (dp, mp + 2 - 4 * y)
    x_id = (dp + 1 - 2 * xi, mp)

    def z_id(d):
        return (base + 2 * lax.rem(zi + d, 4), mp)

    mine, theirs = core * half, (1 - core) * half
    probs, scores_grad = (p0, p1, p2, p3), (s0, s1, s2, s3)

    def remote(src, dst, send, recv, target):
        return pltpu.make_async_remote_copy(
            src_ref=src, dst_ref=dst, send_sem=send, recv_sem=recv, device_id=target, device_id_type=MESH
        )

    def to_core(i, src, dst):
        return remote(src, dst, cs.at[i], cr.at[i], core_id)

    barrier = pltpu.get_barrier_semaphore()
    for target in (core_id, y_id, x_id, z_id(1), z_id(2), z_id(3)):
        pl.semaphore_signal(barrier, inc=1, device_id=target, device_id_type=MESH)
    pl.semaphore_wait(barrier, 6)

    def views(ref, lead, i, part):
        if i < 3:
            return ref.at[(*lead, i, rows_of(part * (shard // 2), shard // 2))]
        if i == 3:
            return ref.at[(*lead, rows_of(part * (shard // 2), shard // 2))]
        quarter = width // 4
        return ref.at[(*lead, rows_of(part * 2 * quarter + ((i - 4) % 2) * quarter, quarter))]

    def buffers(i):
        if i < 3:
            return wqkv_hbm, wqkv
        if i == 3:
            return wout_hbm, wout
        return (wfc_hbm, wfc) if i < 6 else (wproj_hbm, wproj)

    def weight_y(i):
        hbm, vmem = buffers(i)
        return remote(views(hbm, (), i, xi), views(vmem, (1,), i, xi), ws.at[i], wr.at[i], y_id)

    def weight_x(i):
        vmem = buffers(i)[1]
        return remote(views(vmem, (1,), i, xi), views(vmem, (1,), i, xi), fs.at[i], fr.at[i], x_id)

    def weight_own(i):
        hbm, vmem = ((wqkv_hbm, wqkv), (wout_hbm, wout), (wfc_hbm, wfc), (wproj_hbm, wproj))[i]
        return pltpu.make_async_copy(hbm, vmem.at[0], ls.at[i])

    copy_qvb = remote(qvb, qvb_o, ws.at[8], wr.at[8], y_id)
    copy_fcb = remote(fcb, fcb_o, ws.at[9], wr.at[9], y_id)

    def forward(i):
        weight_y(i).wait_recv()
        weight_x(i).start()

    weight_own(0).start()
    copy_qvb.start()
    for i in range(8):
        weight_y(i).start()
    copy_fcb.start()
    for i in range(1, 4):
        weight_own(i).start()

    def n1_copy(i):
        view = n1.at[rows_of(mine + i * BLOCK, BLOCK)]
        return to_core(i, view, view)

    for i in range(half // BLOCK):
        here = pl.ds(i * BLOCK, BLOCK)
        normal, _ = centre(x_ref[here, :].astype(F32))
        n1[rows_of(mine + i * BLOCK, BLOCK), :] = (normal * g1[...] + b1[...]).astype(BF16)
        n1_copy(i).start()
    mg_copy = to_core(2, mg.at[rows_of(mine, half)], mg.at[rows_of(mine, half)])
    total = jnp.zeros((1, width), F32)
    for i in range(half // BLOCK):
        here = pl.ds(i * BLOCK, BLOCK)
        values = cot_ref[here, :].astype(F32)
        mg[rows_of(mine + i * BLOCK, BLOCK), :] = (SCALE * values).astype(BF16)
        total = total + jnp.sum(values, axis=0, keepdims=True)
    mg_copy.start()
    sm_a[...] = jnp.zeros_like(sm_a)
    sm_a[pl.ds(PROJB, 1), :] = SCALE * total

    place = lax.broadcasted_iota(jnp.int32, (rows, 1), 0)
    first = jnp.zeros((rows, 1), jnp.int32)
    end = 0
    slots = docs.shape[1]
    for i in range(slots):
        end = end + docs[y, i]
        first = jnp.where(place >= end, place if i == slots - 1 else end, first)
    lo[...] = first

    def project(s, start, blocks):
        bias = qvb if s == 0 else qvb_o

        def body(m, _):
            here = rows_of(start + m * BLOCK, BLOCK)
            tokens = n1[here, :]
            for j, out in enumerate((qh, kh, vh)):
                t = dot(tokens, wqkv[s, j], NT)
                if j == 0:
                    t = (t + bias[pl.ds(0, 1), :]) * (1.0 / math.sqrt(HD))
                elif j == 2:
                    t = t + bias[pl.ds(1, 1), :]
                t = t.astype(BF16)
                for h in range(nh):
                    out[s * nh + h, here, :] = t[:, h * HD:(h + 1) * HD]
            return 0

        lax.fori_loop(0, blocks, body, 0)

    def attend(s, service):
        def head(t, _):
            service(t)
            h = s * nh + t
            for i in range(nblk):
                seen = BLOCK * (i + 1)
                here = pl.ds(BLOCK * i, BLOCK)
                score = dot(qh[h, here, :], kh[h, pl.ds(0, seen), :], NT)
                key = lax.broadcasted_iota(jnp.int32, (BLOCK, seen), 1)
                query = lax.broadcasted_iota(jnp.int32, (BLOCK, seen), 0) + BLOCK * i
                score = jnp.where((key >= lo[here, :]) & (key <= query), score, -1e30)
                peak = jnp.max(score, axis=-1, keepdims=True)
                exponent = jnp.exp(score - peak)
                scale = 1.0 / jnp.sum(exponent, axis=-1, keepdims=True)
                low = (exponent * scale).astype(BF16)
                probs[i][h] = low
                mxh[h, here, :] = dot(low, vh[h, pl.ds(0, seen), :]).astype(BF16)
            return 0

        lax.fori_loop(0, nh, head, 0)

    weight_own(0).wait()
    project(0, mine, half // BLOCK)
    for i in range(half // BLOCK):
        n1_copy(i).wait_recv()
    project(0, theirs, half // BLOCK)

    def service0(t):
        for i in range(3):
            @pl.when(t == i)
            def _():
                forward(i)

    attend(0, service0)
    copy_qvb.wait_recv()
    forward(3)
    for i in range(3):
        weight_x(i).wait_recv()
    project(1, 0, rows // BLOCK)

    def service1(t):
        for i in range(3):
            @pl.when(t == i)
            def _():
                forward(4 + i)

    attend(1, service1)

    weight_own(1).wait()
    weight_x(3).wait_recv()

    def mixed_of(s, here):
        return jnp.concatenate([mxh[s * nh + h, here, :] for h in range(nh)], axis=1)

    def attn_out(here):
        return dot(mixed_of(0, here), wout[0]) + dot(mixed_of(1, here), wout[1])

    attn_copy = to_core(3, send_a, r_attn)

    def attn_theirs(m, _):
        send_a[rows_of(m * BLOCK, BLOCK), :] = attn_out(rows_of(theirs + m * BLOCK, BLOCK)).astype(BF16)
        return 0

    def attn_mine(m, _):
        here = rows_of(m * BLOCK, BLOCK)
        part = attn_out(rows_of(mine + m * BLOCK, BLOCK))
        hid[here, :] = x_ref[here, :].astype(F32) + SCALE * (part + ob[...])
        return 0

    lax.fori_loop(0, half // BLOCK, attn_theirs, 0)
    attn_copy.start()
    lax.fori_loop(0, half // BLOCK, attn_mine, 0)
    attn_copy.wait()

    def n2_copy(i):
        view = n2.at[rows_of(mine + i * BLOCK, BLOCK)]
        return to_core(4 + i, view, view)

    for i in range(half // BLOCK):
        here = pl.ds(i * BLOCK, BLOCK)
        state = hid[here, :] + SCALE * r_attn[here, :].astype(F32)
        hid[here, :] = state
        normal, _ = centre(state)
        n2[rows_of(mine + i * BLOCK, BLOCK), :] = (normal * g2[...] + b2[...]).astype(BF16)
        n2_copy(i).start()

    def feed(s):
        bias = fcb if s == 0 else fcb_o
        a, b = math.sqrt(2 / math.pi), math.sqrt(2 / math.pi) * 0.044715

        def tile(f, _):
            cols = rows_of(f * BLOCK, BLOCK, BLOCK)
            total = jnp.zeros((1, BLOCK), F32)
            for m in range(2):
                here = pl.ds(half * m, half)
                u = dot(n2[here, :], wfc[s, :, cols]) + bias[:, cols]
                up = dot(mg[here, :], wproj[s, cols, :], NT)
                square = u * u
                th = jnp.tanh(u * (a + b * square))
                low = 0.5 + 0.5 * th
                act_t[s, cols, here] = (u * low).astype(BF16).T
                back = up * (low + (0.5 * u) * (1.0 - th * th) * (a + 3.0 * b * square))
                plo[s, here, cols] = back.astype(BF16)
                total = total + jnp.sum(back, axis=0, keepdims=True)
            sm_a[pl.ds(FCB + 8 * s, 1), cols] = total
            return 0

        lax.fori_loop(0, hidden // BLOCK, tile, 0)

    def grad_proj(s, out):
        def tile(n, _):
            cols = rows_of(n * BLOCK, BLOCK, BLOCK)
            out[pl.ds(0, hidden), cols] = dot(act_t[s], mg[:, cols]).astype(BF16)
            return 0

        lax.fori_loop(0, width // BLOCK, tile, 0)

    def grad_fc(s, out):
        def tile(n, _):
            cols = rows_of(n * BLOCK, BLOCK, BLOCK)
            out[rows_of(hidden + n * BLOCK, BLOCK), :] = dot(plo[s, :, cols], n2[...], TN).astype(BF16)
            return 0

        lax.fori_loop(0, hidden // BLOCK, tile, 0)

    chunk = (2 * hidden + 4 * shard) // CHUNKS
    part, bit = chunk // 2, chunk // 8

    def y_copy(k):
        here = rows_of(k * chunk, chunk)
        there = rows_of(lax.rem(k, 4) * chunk, chunk)
        return remote(g_oth.at[there], y_in.at[here], ys.at[k], yr.at[k], y_id)

    def x_copy(k):
        src = g_own.at[rows_of(k * chunk + (1 - xi) * part, part)]
        return remote(src, x_in.at[rows_of(k * part, part)], xs.at[k], xr.at[k], x_id)

    def z_copy(k, d):
        src = g_own.at[rows_of(k * chunk + xi * part + lax.rem(zi + d, 4) * bit, bit)]
        return remote(src, z_in.at[d - 1, rows_of(k * bit, bit)], zs.at[d - 1, k], zr.at[d - 1, k], z_id(d))

    def place_of(k):
        return grads.at[rows_of(k * chunk + xi * part + zi * bit, bit)]

    def g_copy(k, d):
        src = piece.at[rows_of(k * bit, bit)]
        return remote(src, place_of(k), gs.at[d - 1, k], gr.at[d - 1, k], z_id(d))

    def keep_copy(k):
        return pltpu.make_async_copy(piece.at[rows_of(k * bit, bit)], place_of(k), ks.at[k])

    def e_copy(k):
        view = grads.at[rows_of(k * chunk + xi * part, part)]
        return remote(view, view, es.at[k], er.at[k], x_id)

    def y_done(k):
        y_copy(k).wait_recv()
        step = part // 2

        def add(m, _):
            here = rows_of(k * chunk + m * step, step)
            g_own[here, :] = (g_own[here, :].astype(F32) + y_in[here, :].astype(F32)).astype(BF16)
            return 0

        lax.fori_loop(0, 4, add, 0)
        x_copy(k).start()

    def x_done(k):
        x_copy(k).wait_recv()
        step = part // 2

        def add(m, _):
            here = rows_of(k * chunk + xi * part + m * step, step)
            there = rows_of(k * part + m * step, step)
            g_own[here, :] = (g_own[here, :].astype(F32) + x_in[there, :].astype(F32)).astype(BF16)
            return 0

        lax.fori_loop(0, 2, add, 0)
        for d in (2, 1, 3):
            z_copy(k, d).start()

    def z_done(k):
        for d in (1, 2, 3):
            z_copy(k, d).wait_recv()
        there = rows_of(k * bit, bit)
        total = g_own[rows_of(k * chunk + xi * part + zi * bit, bit), :].astype(F32)
        for d in range(3):
            total = total + z_in[d, there, :].astype(F32)
        piece[there, :] = total.astype(BF16)
        keep_copy(k).start()
        for d in (2, 1, 3):
            g_copy(k, d).start()

    def g_done(k):
        keep_copy(k).wait()
        for d in (1, 2, 3):
            g_copy(k, d).wait_recv()
        e_copy(k).start()

    for i in range(half // BLOCK):
        n2_copy(i).wait_recv()
    mg_copy.wait_recv()
    weight_own(2).wait()
    weight_own(3).wait()
    feed(0)
    forward(7)
    grad_proj(0, g_own)
    grad_fc(0, g_own)
    copy_fcb.wait_recv()
    for i in range(4, 8):
        weight_x(i).wait_recv()
    feed(1)
    grad_proj(1, g_oth)
    y_copy(0).start()
    y_copy(1).start()

    def norm2_part(here, cols):
        return dot(plo[0, here, :], wfc[0, cols, :], NT) + dot(plo[1, here, :], wfc[1, cols, :], NT)

    def norm2_theirs(n, _):
        cols = rows_of(n * BLOCK, BLOCK, BLOCK)
        send_a[:, cols] = norm2_part(rows_of(theirs, half), cols).astype(BF16)
        return 0

    def norm2_mine(n, _):
        cols = rows_of(n * BLOCK, BLOCK, BLOCK)
        hg[:, cols] = norm2_part(rows_of(mine, half), cols)
        return 0

    norm2_copy = to_core(7, send_a, r_n2)
    lax.fori_loop(0, width // BLOCK, norm2_theirs, 0)
    norm2_copy.start()
    lax.fori_loop(0, width // BLOCK, norm2_mine, 0)
    grad_fc(1, g_oth)
    y_copy(2).start()
    y_copy(3).start()
    norm2_copy.wait()

    def ag_copy(i):
        view = ag.at[rows_of(mine + i * BLOCK, BLOCK)]
        return to_core(8 + i, view, view)

    def norm_back(grad, gain, normal, rate):
        n = grad * gain
        return rate * (
            n - jnp.mean(n, axis=-1, keepdims=True) - normal * jnp.mean(n * normal, axis=-1, keepdims=True)
        )

    sums = [jnp.zeros((1, width), F32) for _ in range(3)]
    for i in range(half // BLOCK):
        here = pl.ds(i * BLOCK, BLOCK)
        grad = hg[here, :] + r_n2[here, :].astype(F32)
        normal, rate = centre(hid[here, :])
        state_grad = cot_ref[here, :].astype(F32) + norm_back(grad, g2[...], normal, rate)
        hg[here, :] = state_grad
        ag[rows_of(mine + i * BLOCK, BLOCK), :] = (SCALE * state_grad).astype(BF16)
        ag_copy(i).start()
        for j, value in enumerate((grad * normal, grad, SCALE * state_grad)):
            sums[j] = sums[j] + jnp.sum(value, axis=0, keepdims=True)
    sm_a[pl.ds(LN2G, 1), :] = sums[0]
    sm_a[pl.ds(LN2B, 1), :] = sums[1]
    sm_a[pl.ds(OUTB, 1), :] = sums[2]

    def mlp_part(here, cols):
        return dot(act_t[0, :, here], wproj[0, :, cols], TN) + dot(act_t[1, :, here], wproj[1, :, cols], TN)

    def mlp_theirs(n, _):
        cols = rows_of(n * BLOCK, BLOCK, BLOCK)
        send_b[:, cols] = mlp_part(rows_of(theirs, half, BLOCK), cols).astype(BF16)
        return 0

    def mlp_mine(n, _):
        cols = rows_of(n * BLOCK, BLOCK, BLOCK)
        hid[:, cols] = hid[:, cols] + SCALE * (mlp_part(rows_of(mine, half, BLOCK), cols) + pb[:, cols])
        return 0

    mlp_copy = to_core(6, send_b, r_mlp)
    lax.fori_loop(0, width // BLOCK, mlp_theirs, 0)
    mlp_copy.start()
    lax.fori_loop(0, width // BLOCK, mlp_mine, 0)

    def mixed_grad(start):
        def body(m, _):
            here = rows_of(start + m * BLOCK, BLOCK)
            tokens = ag[here, :]
            for s in range(2):
                t = dot(tokens, wout[s], NT).astype(BF16)
                for h in range(nh):
                    mgh[s * nh + h, here, :] = t[:, h * HD:(h + 1) * HD]
            return 0

        lax.fori_loop(0, half // BLOCK, body, 0)

    mixed_grad(mine)
    for i in range(half // BLOCK):
        ag_copy(i).wait_recv()
    mixed_grad(theirs)

    def grad_out(s, out, start):
        def tile(n, _):
            cols = rows_of(n * BLOCK, BLOCK, BLOCK)
            mixed = mixed_of(s, slice(None))
            out[pl.ds(start, shard), cols] = dot(mixed, ag[:, cols], TN).astype(BF16)
            return 0

        lax.fori_loop(0, width // BLOCK, tile, 0)

    y_copy(0).wait_send()
    y_copy(1).wait_send()
    grad_out(1, g_oth, 0)
    grad_out(0, g_own, 2 * hidden)
    mlp_copy.wait()
    for i in range(half // BLOCK):
        n2_copy(i).wait_send()
        here = pl.ds(i * BLOCK, BLOCK)
        there = rows_of(mine + i * BLOCK, BLOCK)
        n2[there, :] = (hid[here, :] + SCALE * r_mlp[here, :].astype(F32)).astype(BF16)
    result = pltpu.make_async_copy(n2.at[rows_of(mine, half)], layer_out, ks.at[CHUNKS])
    result.start()

    def attend_back(s, service):
        def head(t, _):
            service(t)
            h = s * nh + t
            grad_t, query_t = mgh[h].T, qh[h].T
            for i in range(nblk):
                seen = BLOCK * (i + 1)
                here = pl.ds(BLOCK * i, BLOCK)
                d = mgh[h, here, :]
                inner = jnp.sum(d.astype(F32) * mxh[h, here, :].astype(F32), axis=-1, keepdims=True)
                prob_grad = dot(d, vh[h, pl.ds(0, seen), :], NT)
                ds = (probs[i][h].astype(F32) * (prob_grad - inner)).astype(BF16)
                scores_grad[i][...] = ds
                dq = dot(ds, kh[h, pl.ds(0, seen), :]) * (1.0 / math.sqrt(HD))
                act_t[s, rows_of(t * HD, HD), here] = dq.astype(BF16).T
            for j in range(nblk):
                cols = pl.ds(BLOCK * j, BLOCK)
                value_grad = key_grad = 0.0
                for i in range(j, nblk):
                    there = slice(BLOCK * i, BLOCK * (i + 1))
                    value_grad = value_grad + dot(grad_t[:, there], probs[i][h, :, cols])
                    key_grad = key_grad + dot(query_t[:, there], scores_grad[i][:, cols])
                act_t[s, rows_of(shard + t * HD, HD), cols] = key_grad.astype(BF16)
                act_t[s, rows_of(2 * shard + t * HD, HD), cols] = value_grad.astype(BF16)
            return 0

        lax.fori_loop(0, nh, head, 0)

    def grad_qkv(s, out, start):
        def tile(n, _):
            cols = rows_of(n * BLOCK, BLOCK, BLOCK)
            product = dot(act_t[s, pl.ds(0, 3 * shard), :], n1[:, cols])
            out[pl.ds(start + shard, 3 * shard), cols] = product.astype(BF16)
            return 0

        lax.fori_loop(0, width // BLOCK, tile, 0)

    def service2(t):
        @pl.when(t == 1)
        def _():
            y_done(0)

    attend_back(1, service2)
    grad_qkv(1, g_oth, 0)
    y_copy(4).start()
    y_copy(5).start()

    def service3(t):
        @pl.when(t == 0)
        def _():
            y_done(1)
            x_done(0)

        @pl.when(t == 2)
        def _():
            z_done(0)
            x_done(1)

    attend_back(0, service3)
    grad_qkv(0, g_own, 2 * hidden)

    def norm1_part(here, first):
        total = None
        for s in range(2):
            for j in range(3):
                t = act_t[s, pl.ds(j * shard, shard), here].T
                if j != 1:
                    cols = pl.ds(0 if j == 0 else BLOCK, shard)
                    line = pl.ds(QVB + 8 * s, 1)
                    sm_a[line, cols] = sm_a[line, cols] + jnp.sum(t.astype(F32), axis=0, keepdims=True)
                product = dot(t, wqkv[s, j])
                total = product if total is None else total + product
        return total

    def norm1_theirs(m, _):
        here = rows_of(theirs + m * BLOCK, BLOCK, BLOCK)
        send_b[rows_of(m * BLOCK, BLOCK), :] = norm1_part(here, m == 0).astype(BF16)
        return 0

    def norm1_mine(m, _):
        here = rows_of(mine + m * BLOCK, BLOCK, BLOCK)
        hid[rows_of(m * BLOCK, BLOCK), :] = norm1_part(here, False)
        return 0

    norm1_copy = to_core(10, send_b, r_attn)
    lax.fori_loop(0, half // BLOCK, norm1_theirs, 0)
    norm1_copy.start()
    lax.fori_loop(0, half // BLOCK, norm1_mine, 0)
    y_done(2)
    norm1_copy.wait()
    sums = [jnp.zeros((1, width), F32) for _ in range(2)]
    for i in range(half // BLOCK):
        here = pl.ds(i * BLOCK, BLOCK)
        grad = hid[here, :] + r_attn[here, :].astype(F32)
        normal, rate = centre(x_ref[here, :].astype(F32))
        input_grad[here, :] = (hg[here, :] + norm_back(grad, g1[...], normal, rate)).astype(BF16)
        sums[0] = sums[0] + jnp.sum(grad * normal, axis=0, keepdims=True)
        sums[1] = sums[1] + jnp.sum(grad, axis=0, keepdims=True)
    sm_a[pl.ds(LN1G, 1), :] = sums[0]
    sm_a[pl.ds(LN1B, 1), :] = sums[1]

    small_core = to_core(11, sm_a.at[pl.ds(0, 8)], sm_rc)
    small_core.start()
    y_done(3)
    x_done(2)
    z_done(1)
    g_done(0)
    small_core.wait()
    shared = lax.broadcasted_iota(jnp.int32, (8, width), 0) < FCB
    own, other = sm_a[pl.ds(0, 8), :], sm_a[pl.ds(8, 8), :]
    both = own + sm_rc[...]
    sm_b[pl.ds(0, 8), :] = jnp.where(shared, both, own)
    sm_b[pl.ds(8, 8), :] = jnp.where(shared, both, other)
    small_y = remote(sm_b.at[pl.ds(8, 8)], sm_ry, cs.at[12], cr.at[12], y_id)
    small_y.start()
    y_done(4)
    x_done(3)
    z_done(2)
    g_done(1)
    small_y.wait()
    sm_c[...] = sm_b[pl.ds(0, 8), :] + sm_ry[...]
    small_x = remote(sm_c, sm_rx, cs.at[13], cr.at[13], x_id)
    small_x.start()
    y_done(5)
    x_done(4)
    z_done(3)
    g_done(2)
    small_x.wait()
    sm_d[...] = sm_c[...] + sm_rx[...]
    small_z = [remote(sm_d, sm_rz.at[zi], cs.at[13 + d], cr.at[13 + d], z_id(d)) for d in (1, 2, 3)]
    for copy in small_z:
        copy.start()
    sm_rz[zi] = sm_d[...]
    x_done(5)
    z_done(4)
    g_done(3)
    z_done(5)
    g_done(4)
    for copy in small_z:
        copy.wait()
    small_out[...] = ((sm_rz[0] + sm_rz[1]) + sm_rz[2]) + sm_rz[3]
    g_done(5)

    for k in range(CHUNKS):
        e_copy(k).wait()
        if k > 1:
            y_copy(k).wait_send()
        x_copy(k).wait_send()
        for d in (1, 2, 3):
            z_copy(k, d).wait_send()
            g_copy(k, d).wait_send()
    for i in range(8):
        weight_y(i).wait_send()
        weight_x(i).wait_send()
    copy_qvb.wait_send()
    copy_fcb.wait_send()
    mg_copy.wait_send()
    for i in range(half // BLOCK):
        n1_copy(i).wait_send()
        ag_copy(i).wait_send()
    result.wait()


def shards(
    inputs, cotangent, ln1_gain, ln1_bias, w_qkv, qv_bias, w_out, out_bias, ln2_gain, ln2_bias,
    w_fc, fc_bias, w_proj, proj_bias, doc_lengths,
):
    half, width = inputs.shape
    rows = 2 * half
    shard = w_out.shape[0]
    heads = 2 * (shard // HD)
    hidden = w_proj.shape[0]
    total = 2 * hidden + 4 * shard
    nblk = rows // BLOCK
    vmem = pl.BlockSpec(memory_space=pltpu.VMEM)
    hbm = pl.BlockSpec(memory_space=pl.ANY)
    smem = pl.BlockSpec(memory_space=pltpu.SMEM)

    def low(*shape):
        return pltpu.VMEM(shape, BF16)

    def full(*shape):
        return pltpu.VMEM(shape, F32)

    dma = pltpu.SemaphoreType.DMA
    outs = pl.pallas_call(
        block_kernel,
        out_shape=(
            jax.ShapeDtypeStruct((half, width), BF16),
            jax.ShapeDtypeStruct((half, width), BF16),
            jax.ShapeDtypeStruct((total, width), BF16),
            jax.ShapeDtypeStruct((8, width), F32),
        ),
        in_specs=[vmem, vmem, vmem, vmem, hbm, vmem, hbm, vmem, vmem, vmem, hbm, vmem, hbm, vmem, smem],
        out_specs=(hbm, vmem, hbm, vmem),
        scratch_shapes=[
            low(2, 3, shard, width), low(2, shard, width), low(2, width, hidden), low(2, hidden, width),
            full(2, shard), full(1, hidden),
            low(rows, width), low(rows, width), low(rows, width), low(rows, width),
            *[low(heads, rows, HD) for _ in range(5)],
            *[low(heads, BLOCK, BLOCK * (i + 1)) for i in range(nblk)],
            *[low(BLOCK, BLOCK * (i + 1)) for i in range(nblk)],
            low(2, hidden, rows), low(2, rows, hidden), full(half, width), full(half, width),
            *[low(half, width) for _ in range(5)],
            low(total, width), low(2 * hidden, width), low(total, width), low(total // 2, width),
            low(3, total // 8, width), low(total // 8, width),
            pltpu.VMEM((rows, 1), jnp.int32),
            full(16, width), full(16, width), full(8, width), full(8, width),
            full(8, width), full(8, width), full(8, width), full(4, 8, width),
            dma((17,)), dma((17,)), dma((10,)), dma((10,)), dma((8,)), dma((8,)), dma((4,)),
            dma((CHUNKS,)), dma((CHUNKS,)), dma((CHUNKS,)), dma((CHUNKS,)),
            dma((3, CHUNKS)), dma((3, CHUNKS)), dma((3, CHUNKS)), dma((3, CHUNKS)),
            dma((CHUNKS,)), dma((CHUNKS,)), dma((CHUNKS + 1,)),
        ],
        compiler_params=pltpu.CompilerParams(
            collective_id=0, has_side_effects=True, vmem_limit_bytes=66_000_000
        ),
        name="block",
    )(
        inputs, cotangent, ln1_gain[None], ln1_bias[None], w_qkv.transpose(0, 2, 1), qv_bias, w_out, out_bias[None],
        ln2_gain[None], ln2_bias[None], w_fc, fc_bias[None], w_proj, proj_bias[None], doc_lengths,
    )
    layer_out, input_grad, grads, small = outs
    grads = grads.astype(F32)
    count = lax.axis_size("dp")
    if count > 8:
        groups = [[g * 8 + i for g in range(count // 8)] for i in range(8)]
        grads, small = lax.psum((grads, small), "dp", axis_index_groups=groups)
    proj_grad, fc_grad = grads[:hidden], grads[hidden:2 * hidden].T
    out_grad = grads[2 * hidden:2 * hidden + shard]
    qkv_grad = grads[2 * hidden + shard:].reshape(3, shard, width).transpose(0, 2, 1)
    qv_grad = jnp.stack([small[QVB, :shard], small[QVB, BLOCK:BLOCK + shard]])
    return (
        layer_out, input_grad, small[LN1G], small[LN1B], qkv_grad, qv_grad, out_grad, small[OUTB],
        small[LN2G], small[LN2B], fc_grad, small[FCB, :hidden], proj_grad, small[PROJB],
    )


def solution(mesh):
    tokens = P(("dp", "mp"), None)
    in_specs = (
        tokens, tokens, P(), P(), P(None, None, "mp"), P(None, "mp"), P("mp", None), P(), P(), P(),
        P(None, "mp"), P("mp"), P("mp", None), P(), P("dp", None),
    )
    out_specs = (
        tokens, tokens, P(), P(), P(None, None, "mp"), P(None, "mp"), P("mp", None), P(), P(), P(),
        P(None, "mp"), P("mp"), P("mp", None), P(),
    )
    return jax.shard_map(shards, mesh=mesh, in_specs=in_specs, out_specs=out_specs, check_vma=False)
```

time: 911 us -> 221 us (0.24)
  waiting for transfers between devices: 498 us -> 0 us
  Pallas kernels: 0 us -> 195 us
  matrix products: 165 us -> 0 us
  other arithmetic: 87.4 us -> 3.13 us
  blocking collectives: 65.2 us -> 0 us
  local copies, waits for them, and re-layouts: 74.8 us -> 21.5 us
  between operations: 14.9 us -> 0.67 us
    pallas_call x0 -> x1, Pallas kernels: none -> 195 us  [shards(): pl.pallas_call(block_kernel, out_shape=(jax.ShapeDtypeStruct((half, width...]
    psum x1 -> x0, waiting for transfers between devices: 180 us -> none  [shards(): lax.psum((qkv_grad, qv_bias_grad, out_weight_grad, fc_weight_grad, fc_bia...]
    all_gather x6 -> x0, waiting for transfers between devices: 167 us -> none  [the longest x2 59.5 us: front(): normed1_all = lax.all_gather(normed1, 'mp', axis=0, tiled=True)]
    reduce_scatter x5 -> x0, waiting for transfers between devices: 151 us -> none  [the longest x2 76.1 us: front(): lax.psum_scatter(jnp.dot(mixed, w_out, preferred_element_type=jnp.float32...]
    dot_general x28 -> x0, matrix products: 136 us -> none  [the longest x4 27 us: one_row(): jnp.einsum('hqk,khd->qhd', probs.astype(jnp.bfloat16), value_row, preferr...]
    psum x2 -> x0, blocking collectives: 65.2 us -> none  [the longest x1 42.6 us: shards(): lax.psum((ln1_gain_grad, ln1_bias_grad, out_bias_grad, ln2_gain_grad, ln2...]
    reduce_sum x16 -> x0, other arithmetic: 34.4 us -> none  [the longest x2 14.8 us: one_row(): total = jnp.sum(exponent, axis=-1, keepdims=True)]
    convert_element_type x12 -> x1, other arithmetic: 34.5 us -> 2.54 us  [shards(): grads = grads.astype(F32)]
  transfers between devices with their start and end apart: 12 -> 0, of which waited for: 11 -> 0; matrix products, arithmetic and copies ran while one was open for 5% -> 0% of each run, Pallas kernels for 0% -> 0%
where the time goes in v1:
time: 221 us
  Pallas kernels  195 us (88%)
  local copies, waits for them, and re-layouts  21.5 us (10%)
  other arithmetic  3.13 us (1%)
    pallas_call x1, Pallas kernels, shards(): pl.pallas_call(block_kernel, out_shape=(jax.ShapeDtypeStruct((half, width...  195 us
    unnamed x9, local copies, waits for them, and re-layouts  4.96 us

profile of v1, /device:TPU:0, one launch (start us, length us, event | category | flops | bytes accessed | tf_op | source)
XLA Modules:
  0.0 220.6 jit_solution(12579973317940618835)
XLA Ops:
  0.6 1.3 broadcast_in_dim.21.g1
  1.9 1.3 broadcast_in_dim.22.b1
  3.2 1.3 broadcast_in_dim.23.ob
  4.4 1.3 broadcast_in_dim.24.g2
  5.7 1.3 broadcast_in_dim.25.b2
  7.0 1.3 broadcast_in_dim.26.fcb
  8.2 1.3 broadcast_in_dim.27.pb
  9.5 195.3 %block.1 = (bf16[512,768]{1,0:T(8,128)(2,1)}, bf16[512,768]{1,0:T(8,128)(2,1)}, bf16[2304,768]{1,0:T(8,128)(2,1)}, f32[8,768]{1,0:T(8,128)}) custom-call(bf16[512,768]{1,0:T(8,128)(2,1)} %x_ref.1, bf16[512,768]{1,0:T(8,128)(2,1)} %cot_ref.1, f32[1,768]{1,0:T(1,128)} %broadcast_in_dim.21.g1, f32[1,768]{1,0:T(1,128)} %broadcast_in_dim.22.b1, ...), custom_call_target="tpu_custom_call" | custom-call | tf_op jit(solution)/shard_map/block/pallas_call | solution.py:677
  204.8 0.7 fusion
  205.5 0.6 pad_maximum_fusion
  206.1 1.7 slice_reduce_fusion
  207.8 2.5 %convert_element_type.3 = f32[2304,768]{1,0:T(8,128)S(1)} convert(bf16[2304,768]{1,0:T(8,128)(2,1)} %get-tuple-element.21) | non-fusion elementwise | flops 1769472 | bytes 10616832 | tf_op jit(solution)/shard_map/convert_element_type | solution.py:715
  210.3 1.6 slice_bitcast_fusion
  211.9 0.0 copy-start
  211.9 3.2 %copy.29 = f32[768,768]{1,0:T(8,128)} copy(f32[768,768]{0,1:T(8,128)} %slice_bitcast_fusion) | data formatting | bytes 4718592
  215.1 0.0 copy-done
  215.1 1.6 slice.55
  216.7 0.0 copy-start.2
  216.7 1.3 slice.52
  218.0 0.9 slice.53
  218.9 0.0 copy-done.2
  218.9 0.9 copy.32
  219.8 0.0 copy-done.1
  219.8 0.9 copy.33
  (1 shorter events, 0.0 us)
Async XLA Ops:
  211.9 3.2 %copy-start = (bf16[2304,768]{1,0:T(8,128)(2,1)S(1)}, bf16[2304,768]{1,0:T(8,128)(2,1)}, u32[]{:S(2)}) copy-start(bf16[2304,768]{1,0:T(8,128)(2,1)} %get-tuple-element.21) | copy-start | bytes 10616836
  216.7 2.2 copy-start.2
  216.7 3.1 %copy-start.1 = (bf16[512,768]{1,0:T(8,128)(2,1)S(1)}, bf16[512,768]{1,0:T(8,128)(2,1)}, u32[]{:S(2)}) copy-start(bf16[512,768]{1,0:T(8,128)(2,1)} %get-tuple-element.60) | copy-start | bytes 2359300

commit v2 on v1

v2 whole, which is shorter than its diff:
```python
import math

import jax
import jax.numpy as jnp
from jax import lax
from jax.experimental import pallas as pl
from jax.experimental.pallas import tpu as pltpu
from jax.sharding import PartitionSpec as P

HD = 64
SCALE = 12 ** (-0.5)
MESH = pl.DeviceIdType.MESH
F32 = jnp.float32
BF16 = jnp.bfloat16
NN = (((1,), (0,)), ((), ()))
NT = (((1,), (1,)), ((), ()))
TN = (((0,), (0,)), ((), ()))
BLOCK = 256
LN1G, LN1B, OUTB, LN2G, LN2B, PROJB, FCB, QVB = range(8)
ORDERS = (
    ("y", "x", "z2", "z1"),
    ("z1", "y", "x", "z2"),
    ("x", "y", "z1", "z2"),
    ("z1", "y", "x", "z2"),
    ("x", "y", "z1", "z2"),
    ("z1", "y", "x", "z2"),
    ("z1", "y", "x", "z2"),
    ("x", "y", "z2", "z1"),
    ("y", "x", "z1", "z2"),
)
ROUTES = ("z1", "x", "z1", "x", "z1", "x", "z1", "x")
SENDS = (0, 1, 2, 3, 4, 5, 6, 7)
SCHEDULE = {
    "att0.0.0": (("w", 0, 0),),
    "att0.0.1": (("w", 1, 0),),
    "att0.3.1": (("w", 2, 0),),
    "att0.1.2": (("w", 0, 1),),
    "needqkv": (("w", 1, 1), ("w", 2, 1), ("w", 3, 0), ("w", 4, 0), ("w", 5, 0),),
    "att1.0.0": (("w", 3, 1), ("w", 6, 0),),
    "att1.0.1": (("w", 4, 1),),
    "att1.2.1": (("w", 7, 0),),
    "att1.3.2": (("w", 5, 1),),
    "ln2": (("w", 6, 1),),
    "feed0.2": (("w", 7, 1),),
    "mixb": (("g", 2, 0), ("g", 0, 0), ("g", 1, 0),),
    "gq1.0": (("g", 4, 0), ("g", 3, 0),),
    "gq0.0": (("g", 2, 1),),
    "ab1.1": (("g", 0, 1), ("g", 5, 0),),
    "gq0.1": (("g", 1, 1),),
    "ab0.2": (("g", 2, 2), ("g", 4, 1),),
    "mlpa.0": (("g", 6, 0), ("g", 3, 1),),
    "mlpa.1": (("g", 1, 2),),
    "ln1b.0": (("g", 0, 2),),
    "ln1b.1": (("g", 2, 3), ("g", 5, 1), ("g", 7, 0), ("g", 4, 2),),
    "mlpb.0": (("g", 3, 2), ("g", 1, 3), ("g", 0, 3),),
    "mlpb.2": (("s", 0),),
    "out": (("g", 5, 2),),
    "end": (("g", 2, 4), ("g", 4, 3), ("g", 8, 0), ("g", 0, 4), ("g", 3, 3), ("g", 2, 5), ("g", 1, 4), ("g", 6, 1), ("g", 5, 3), ("g", 8, 1), ("g", 4, 4), ("g", 7, 1), ("s", 1), ("g", 2, 6), ("g", 8, 2), ("g", 0, 5), ("g", 1, 5), ("g", 4, 5), ("g", 3, 4), ("g", 6, 2), ("s", 2), ("g", 5, 4), ("g", 0, 6), ("g", 7, 2), ("g", 1, 6), ("g", 8, 3), ("s", 3), ("g", 4, 6), ("g", 7, 3), ("g", 6, 3), ("g", 3, 5), ("g", 8, 4), ("g", 7, 4), ("g", 5, 5), ("s", 4), ("g", 6, 4), ("g", 3, 6), ("g", 8, 5), ("g", 6, 5), ("g", 7, 5), ("g", 5, 6), ("g", 8, 6), ("g", 6, 6), ("g", 7, 6),),
}


def dot(a, b, dims=NN):
    return lax.dot_general(a, b, dims, preferred_element_type=F32)


def rows_of(start, size, align=16):
    return pl.ds(pl.multiple_of(start, align), size)


def centre(values):
    average = jnp.mean(values, axis=-1, keepdims=True)
    centred = values - average
    spread = jnp.mean(centred * centred, axis=-1, keepdims=True)
    rate = lax.rsqrt(spread + 1e-05)
    return centred * rate, rate


def norm_back(grad, gain, normal, rate):
    n = grad * gain
    return rate * (n - jnp.mean(n, axis=-1, keepdims=True) - normal * jnp.mean(n * normal, axis=-1, keepdims=True))


def line(ref):
    return ref[...].reshape(1, -1)


def block_kernel(
    x_ref, cot_ref, g1, b1, wqkv_hbm, qvb, wout_hbm, ob, g2, b2, wfc_hbm, fcb, wproj_hbm, pb, docs,
    layer_out, input_grad, f_proj, f_fc, f_att, small_out,
    wqkv, wout, wfc, wproj, qvb_o, fcb_o, n1, n2, mg, ag, qh, kh, vh, mxh, mgh, p0, p1, p2, p3,
    s0, s1, s2, s3, dq, act_t, plo, hid, hg, send_a, r_attn, r_n2,
    g_own, g_oth, r_buf, lo, sm_a, sm_b, sm_c, sm_r,
    cs, cr, ws, wr, ls, gs, gr, ks,
):
    half, width = x_ref.shape
    rows = 2 * half
    shard = wout_hbm.shape[0]
    nh = shard // HD
    hidden = wproj_hbm.shape[0]
    nblk = rows // BLOCK
    hblk = half // BLOCK
    dp, mp = lax.axis_index("dp"), lax.axis_index("mp")
    core, y = lax.rem(mp, 2), lax.div(mp, 2)
    bits = {
        "y": y,
        "x": lax.rem(dp, 2),
        "z1": lax.rem(lax.div(dp, 2), 2),
        "z2": lax.rem(lax.div(dp, 4), 2),
    }
    targets = {
        "core": (dp, mp + 1 - 2 * core),
        "y": (dp, mp + 2 - 4 * y),
        "x": (dp + 1 - 2 * bits["x"], mp),
        "z1": (dp + 2 - 4 * bits["z1"], mp),
        "z2": (dp + 4 - 8 * bits["z2"], mp),
    }
    mine, theirs = core * half, (1 - core) * half
    probs, scores_grad = (p0, p1, p2, p3), (s0, s1, s2, s3)

    def remote(src, dst, send, recv, axis):
        return pltpu.make_async_remote_copy(
            src_ref=src, dst_ref=dst, send_sem=send, recv_sem=recv, device_id=targets[axis], device_id_type=MESH
        )

    def to_core(i, src, dst):
        return remote(src, dst, cs.at[i], cr.at[i], "core")

    barrier = pltpu.get_barrier_semaphore()
    for target in targets.values():
        pl.semaphore_signal(barrier, inc=1, device_id=target, device_id_type=MESH)
    pl.semaphore_wait(barrier, len(targets))

    group = bits["x"] + 2 * bits["z1"]
    beside = {"x": group + 1 - 2 * bits["x"], "z1": group + 2 - 4 * bits["z1"]}

    def slot_piece(ref, lead, j, index):
        if j < 3:
            return ref.at[(*lead, j, rows_of(index * (shard // 4), shard // 4))]
        if j == 3:
            return ref.at[(*lead, rows_of(index * (shard // 4), shard // 4))]
        size = width // 8
        return ref.at[(*lead, rows_of((j % 2) * 4 * size + index * size, size))]

    def slot_refs(j):
        if j < 3:
            return wqkv_hbm, wqkv
        if j == 3:
            return wout_hbm, wout
        return (wfc_hbm, wfc) if j < 6 else (wproj_hbm, wproj)

    def weight_copy(j, way):
        hbm, vmem = slot_refs(j)
        number = ("y", "x", "z1", "last").index(way)
        if way == "y":
            src, dst, axis = slot_piece(hbm, (), j, group), slot_piece(vmem, (1,), j, group), "y"
        else:
            axis = ROUTES[j] if way == "last" else way
            index = group if way != "last" else beside["x" if axis == "z1" else "z1"]
            src = dst = slot_piece(vmem, (1,), j, index)
        return remote(src, dst, ws.at[number, j], wr.at[number, j], axis)

    def weight_own(i):
        hbm, vmem = ((wqkv_hbm, wqkv), (wout_hbm, wout), (wfc_hbm, wfc), (wproj_hbm, wproj))[i]
        return pltpu.make_async_copy(hbm, vmem.at[0], ls.at[i])

    copy_qvb = remote(qvb, qvb_o, ws.at[0, 8], wr.at[0, 8], "y")
    copy_fcb = remote(fcb, fcb_o, ws.at[0, 9], wr.at[0, 9], "y")
    arrived = set()

    def weight_step(j, hop):
        if hop == 0:
            weight_copy(j, "y").wait_recv()
            weight_copy(j, "x").start()
            weight_copy(j, "z1").start()
        else:
            way = "x" if ROUTES[j] == "z1" else "z1"
            weight_copy(j, way).wait_recv()
            arrived.add((j, way))
            weight_copy(j, "last").start()

    def need(slots):
        for j in slots:
            for way in ("x", "z1", "last"):
                if (j, way) not in arrived:
                    weight_copy(j, way).wait_recv()

    each = BLOCK + BLOCK // 2 + BLOCK // 4 + BLOCK // 8
    stages = []
    for k, order in enumerate(ORDERS):
        offset, size, at, whole, plan = k * BLOCK, BLOCK, k * each, True, []
        for axis in order:
            if axis == "y":
                plan.append((axis, offset, offset, size, at, False))
                at, whole = at + size, False
            else:
                size //= 2
                keep, give = offset + bits[axis] * size, offset + (1 - bits[axis]) * size
                plan.append((axis, keep, give, size, at, whole))
                at, offset = at + size * (2 if whole else 1), keep
        stages.append(plan)

    def grad_copies(k, stage, only=(True, True)):
        axis, _, give, size, at, whole = stages[k][stage]
        parts = []
        if axis != "y":
            parts.append((g_own, 0))
        if axis == "y" or whole:
            parts.append((g_oth, len(parts)))
        parts = [part for part in parts if only[part[0] is g_oth]]
        return [
            remote(
                ref.at[rows_of(give, size)], r_buf.at[rows_of(at + i * size, size)],
                gs.at[k, 2 * stage + i], gr.at[k, 2 * stage + i], axis,
            )
            for ref, i in parts
        ]

    results = (f_proj, f_fc, f_att)

    def result_rows(k, start, size):
        return results[k // 3].at[rows_of(start - (k // 3) * 3 * BLOCK, size)]

    def gather_plan(k):
        return [entry for entry in reversed(stages[k]) if entry[0] != "y"]

    def gather_copy(k, i):
        plan = gather_plan(k)
        start, size = plan[i][1], plan[i][3]
        src = g_own.at[rows_of(start, size)] if i == 0 else result_rows(k, start, size)
        return remote(src, result_rows(k, start, size), gs.at[k, 8 + i], gr.at[k, 8 + i], plan[i][0])

    def keep_copy(k):
        start, size = gather_plan(k)[0][1], gather_plan(k)[0][3]
        return pltpu.make_async_copy(g_own.at[rows_of(start, size)], result_rows(k, start, size), ks.at[k])

    def add(ref, start, size, at):
        step = min(size, BLOCK // 4)

        def body(m, _):
            here, there = rows_of(start + m * step, step), rows_of(at + m * step, step)
            ref[here, :] = (ref[here, :].astype(F32) + r_buf[there, :].astype(F32)).astype(BF16)
            return 0

        if size == step:
            body(0, 0)
        else:
            lax.fori_loop(0, size // step, body, 0)

    def grad_step(k, stage):
        if stage < len(stages[k]):
            axis, keep, _, size, at, whole = stages[k][stage]
            for copy in grad_copies(k, stage):
                copy.wait_recv()
            add(g_own, keep, size, at)
            if whole:
                add(g_oth, keep, size, at + size)
            if stage + 1 < len(stages[k]):
                for copy in grad_copies(k, stage + 1):
                    copy.start()
            else:
                keep_copy(k).start()
                gather_copy(k, 0).start()
        else:
            i = stage - len(stages[k])
            gather_copy(k, i).wait_recv()
            if i == 0:
                keep_copy(k).wait()
            if i < 2:
                gather_copy(k, i + 1).start()

    def grad_ready(k, other):
        for copy in grad_copies(k, 0, (not other, other)):
            copy.start()

    def ready_at(first, t, s):
        for i in range(3):
            if s == 1 or ORDERS[first + i][0] != "y":
                pl.when(t == i)(lambda i=i: grad_ready(first + i, s == 1))

    ways = ("core", "y", "x", "z1", "z2")

    def small_copy(i):
        src = (sm_a.at[pl.ds(0, 8)], sm_b.at[pl.ds(8, 8)], sm_c.at[0], sm_c.at[1], sm_c.at[2])[i]
        return remote(src, sm_r.at[i], cs.at[11 + i], cr.at[11 + i], ways[i])

    def small_step(i):
        small_copy(i).wait()
        if i == 0:
            shared = lax.broadcasted_iota(jnp.int32, (8, width), 0) < FCB
            own, other = sm_a[pl.ds(0, 8), :], sm_a[pl.ds(8, 8), :]
            both = own + sm_r[0]
            sm_b[pl.ds(0, 8), :] = jnp.where(shared, both, own)
            sm_b[pl.ds(8, 8), :] = jnp.where(shared, both, other)
        elif i < 4:
            sm_c[i - 1] = (sm_b[pl.ds(0, 8), :] if i == 1 else sm_c[i - 2]) + sm_r[i]
        else:
            small_out[...] = sm_c[2] + sm_r[4]
        if i < 4:
            small_copy(i + 1).start()

    def service(point):
        for kind, *where in SCHEDULE.get(point, ()):
            {"w": weight_step, "g": grad_step, "s": small_step}[kind](*where)

    def service_at(point, t, count):
        for i in range(count):
            if f"{point}.{i}" in SCHEDULE:
                pl.when(t == i)(lambda i=i: service(f"{point}.{i}"))

    weight_own(0).start()
    copy_qvb.start()
    for j in SENDS:
        weight_copy(j, "y").start()
    copy_fcb.start()
    for i in range(1, 4):
        weight_own(i).start()

    def n1_copy(i):
        view = n1.at[rows_of(mine + i * BLOCK, BLOCK)]
        return to_core(i, view, view)

    for i in range(hblk):
        here = pl.ds(i * BLOCK, BLOCK)
        normal, _ = centre(x_ref[here, :].astype(F32))
        n1[rows_of(mine + i * BLOCK, BLOCK), :] = (normal * line(g1) + line(b1)).astype(BF16)
        n1_copy(i).start()

    def project(s, start, blocks):
        bias = qvb if s == 0 else qvb_o

        def body(m, _):
            here = rows_of(start + m * BLOCK, BLOCK)
            tokens = n1[here, :]
            for j, out in enumerate((qh, kh, vh)):
                t = dot(tokens, wqkv[s, j], NT)
                if j == 0:
                    t = (t + bias[pl.ds(0, 1), :]) * (1.0 / math.sqrt(HD))
                elif j == 2:
                    t = t + bias[pl.ds(1, 1), :]
                t = t.astype(BF16)
                for h in range(nh):
                    out[s * nh + h, here, :] = t[:, h * HD:(h + 1) * HD]
            return 0

        lax.fori_loop(0, blocks, body, 0)

    def first_keys():
        place = lax.broadcasted_iota(jnp.int32, (rows, 1), 0)
        first = jnp.zeros((rows, 1), jnp.int32)
        end = 0
        slots = docs.shape[1]
        for i in range(slots):
            end = end + docs[y, i]
            first = jnp.where(place >= end, place if i == slots - 1 else end, first)
        lo[...] = first

    def attend(s):
        def head(t, _):
            h = s * nh + t
            for i in range(nblk):
                service_at(f"att{s}.{i}", t, nh)
                seen = BLOCK * (i + 1)
                here = pl.ds(BLOCK * i, BLOCK)
                score = dot(qh[h, here, :], kh[h, pl.ds(0, seen), :], NT)
                key = lax.broadcasted_iota(jnp.int32, (BLOCK, seen), 1)
                query = lax.broadcasted_iota(jnp.int32, (BLOCK, seen), 0) + BLOCK * i
                score = jnp.where((key >= lo[here, :]) & (key <= query), score, -1e30)
                peak = jnp.max(score, axis=-1, keepdims=True)
                exponent = jnp.exp(score - peak)
                scale = 1.0 / jnp.sum(exponent, axis=-1, keepdims=True)
                low = (exponent * scale).astype(BF16)
                probs[i][h] = low
                mxh[h, here, :] = dot(low, vh[h, pl.ds(0, seen), :]).astype(BF16)
            return 0

        lax.fori_loop(0, nh, head, 0)

    weight_own(0).wait()
    service("qkv0a")
    project(0, mine, hblk)
    service("qkv0b")
    for i in range(hblk):
        n1_copy(i).wait_recv()
    project(0, theirs, hblk)
    first_keys()
    attend(0)

    service("mg")
    mg_copy = to_core(2, mg.at[rows_of(mine, half)], mg.at[rows_of(mine, half)])
    total = jnp.zeros((1, width), F32)
    for i in range(hblk):
        values = cot_ref[pl.ds(i * BLOCK, BLOCK), :].astype(F32)
        mg[rows_of(mine + i * BLOCK, BLOCK), :] = (SCALE * values).astype(BF16)
        total = total + jnp.sum(values, axis=0, keepdims=True)
    mg_copy.start()
    sm_a[...] = jnp.zeros_like(sm_a)
    sm_a[pl.ds(PROJB, 1), :] = SCALE * total

    service("needqkv")
    copy_qvb.wait_recv()
    need(range(3))
    service("qkv1a")
    project(1, 0, hblk)
    service("qkv1b")
    project(1, half, hblk)
    attend(1)

    service("needout")
    weight_own(1).wait()
    need(range(3, 4))

    def mixed_of(s, here):
        return jnp.concatenate([mxh[s * nh + h, here, :] for h in range(nh)], axis=1)

    def attn_out(here):
        return dot(mixed_of(0, here), wout[0]) + dot(mixed_of(1, here), wout[1])

    attn_copy = to_core(3, send_a, r_attn)

    def attn_theirs(m, _):
        send_a[rows_of(m * BLOCK, BLOCK), :] = attn_out(rows_of(theirs + m * BLOCK, BLOCK)).astype(BF16)
        return 0

    def attn_mine(m, _):
        here = rows_of(m * BLOCK, BLOCK)
        part = attn_out(rows_of(mine + m * BLOCK, BLOCK))
        hid[here, :] = x_ref[here, :].astype(F32) + SCALE * (part + line(ob))
        return 0

    service("outa")
    lax.fori_loop(0, hblk, attn_theirs, 0)
    attn_copy.start()
    service("outb")
    lax.fori_loop(0, hblk, attn_mine, 0)
    attn_copy.wait()

    def n2_copy(i):
        view = n2.at[rows_of(mine + i * BLOCK, BLOCK)]
        return to_core(4 + i, view, view)

    for i in range(hblk):
        here = pl.ds(i * BLOCK, BLOCK)
        state = hid[here, :] + SCALE * r_attn[here, :].astype(F32)
        hid[here, :] = state
        normal, _ = centre(state)
        n2[rows_of(mine + i * BLOCK, BLOCK), :] = (normal * line(g2) + line(b2)).astype(BF16)
        n2_copy(i).start()

    def feed(s):
        bias = line(fcb if s == 0 else fcb_o)
        a, b = math.sqrt(2 / math.pi), math.sqrt(2 / math.pi) * 0.044715
        out = g_own if s == 0 else g_oth

        def tile(f, _):
            service_at(f"feed{s}", f, hidden // BLOCK)
            cols = rows_of(f * BLOCK, BLOCK, BLOCK)
            total = jnp.zeros((1, BLOCK), F32)
            for m in range(2):
                here = pl.ds(half * m, half)
                u = dot(n2[here, :], wfc[s, :, cols]) + (fcb if s == 0 else fcb_o)[cols].reshape(1, -1)
                up = dot(mg[here, :], wproj[s, cols, :], NT)
                square = u * u
                th = jnp.tanh(u * (a + b * square))
                low = 0.5 + 0.5 * th
                act_t[s, cols, here] = (u * low).astype(BF16).T
                back = up * (low + (0.5 * u) * (1.0 - th * th) * (a + 3.0 * b * square))
                plo[s, here, cols] = back.astype(BF16)
                total = total + jnp.sum(back, axis=0, keepdims=True)
            sm_a[pl.ds(FCB + 8 * s, 1), cols] = total
            out[rows_of(f * BLOCK, BLOCK), :] = dot(act_t[s, cols, :], mg[...]).astype(BF16)
            ready_at(0, f, s)
            return 0

        lax.fori_loop(0, hidden // BLOCK, tile, 0)

    def grad_fc(s):
        out = g_own if s == 0 else g_oth

        def tile(n, _):
            service_at(f"gfc{s}", n, width // BLOCK)
            cols = rows_of(n * BLOCK, BLOCK, BLOCK)
            out[rows_of(hidden + n * BLOCK, BLOCK), :] = dot(n2[:, cols], plo[s], TN).astype(BF16)
            ready_at(3, n, s)
            return 0

        lax.fori_loop(0, width // BLOCK, tile, 0)

    service("ln2")
    for i in range(hblk):
        n2_copy(i).wait_recv()
    mg_copy.wait_recv()
    weight_own(2).wait()
    weight_own(3).wait()
    feed(0)
    grad_fc(0)
    service("needfp")
    copy_fcb.wait_recv()
    need(range(4, 8))
    feed(1)

    def norm2_part(here, cols):
        return dot(plo[0, here, :], wfc[0, cols, :], NT) + dot(plo[1, here, :], wfc[1, cols, :], NT)

    def norm2_theirs(n, _):
        cols = rows_of(n * BLOCK, BLOCK, BLOCK)
        send_a[:, cols] = norm2_part(rows_of(theirs, half), cols).astype(BF16)
        return 0

    def norm2_mine(n, _):
        cols = rows_of(n * BLOCK, BLOCK, BLOCK)
        hg[:, cols] = norm2_part(rows_of(mine, half), cols)
        return 0

    norm2_copy = to_core(7, send_a, r_n2)
    service("n2a")
    lax.fori_loop(0, width // BLOCK, norm2_theirs, 0)
    norm2_copy.start()
    service("n2b")
    lax.fori_loop(0, width // BLOCK, norm2_mine, 0)
    grad_fc(1)
    service("ln2b")
    norm2_copy.wait()

    def ag_copy(i):
        view = ag.at[rows_of(mine + i * BLOCK, BLOCK)]
        return to_core(8 + i, view, view)

    sums = [jnp.zeros((1, width), F32) for _ in range(3)]
    for i in range(hblk):
        here = pl.ds(i * BLOCK, BLOCK)
        grad = hg[here, :] + r_n2[here, :].astype(F32)
        normal, rate = centre(hid[here, :])
        state_grad = cot_ref[here, :].astype(F32) + norm_back(grad, line(g2), normal, rate)
        hg[here, :] = state_grad
        ag[rows_of(mine + i * BLOCK, BLOCK), :] = (SCALE * state_grad).astype(BF16)
        ag_copy(i).start()
        for j, value in enumerate((grad * normal, grad, SCALE * state_grad)):
            sums[j] = sums[j] + jnp.sum(value, axis=0, keepdims=True)
    sm_a[pl.ds(LN2G, 1), :] = sums[0]
    sm_a[pl.ds(LN2B, 1), :] = sums[1]
    sm_a[pl.ds(OUTB, 1), :] = sums[2]

    def mixed_grad(start):
        def body(m, _):
            here = rows_of(start + m * BLOCK, BLOCK)
            tokens = ag[here, :]
            for s in range(2):
                t = dot(tokens, wout[s], NT).astype(BF16)
                for h in range(nh):
                    mgh[s * nh + h, here, :] = t[:, h * HD:(h + 1) * HD]
            return 0

        lax.fori_loop(0, hblk, body, 0)

    service("mixa")
    mixed_grad(mine)
    for i in range(hblk):
        ag_copy(i).wait_recv()
    service("mixb")
    mixed_grad(theirs)

    def grad_out(s):
        out = g_own if s == 0 else g_oth

        def tile(n, _):
            cols = rows_of(n * BLOCK, BLOCK, BLOCK)
            product = dot(mixed_of(s, slice(None)), ag[:, cols], TN).astype(BF16)
            for h in range(nh):
                out[pl.ds(2 * hidden + h * BLOCK, HD), cols] = product[h * HD:(h + 1) * HD]
            return 0

        lax.fori_loop(0, width // BLOCK, tile, 0)

    service("gout")
    grad_out(1)
    grad_out(0)

    def head_back(s, t):
        h = s * nh + t
        first = rows_of(t * BLOCK, BLOCK, BLOCK)
        grad_t, query_t = mgh[h].T, qh[h].T
        for i in range(nblk):
            seen = BLOCK * (i + 1)
            here = pl.ds(BLOCK * i, BLOCK)
            d = mgh[h, here, :]
            inner = jnp.sum(d.astype(F32) * mxh[h, here, :].astype(F32), axis=-1, keepdims=True)
            prob_grad = dot(d, vh[h, pl.ds(0, seen), :], NT)
            ds = (probs[i][h].astype(F32) * (prob_grad - inner)).astype(BF16)
            scores_grad[i][...] = ds
            dq[here, :] = (dot(ds, kh[h, pl.ds(0, seen), :]) * (1.0 / math.sqrt(HD))).astype(BF16)
        for j in range(nblk):
            cols = pl.ds(BLOCK * j, BLOCK)
            value_grad = key_grad = 0.0
            for i in range(j, nblk):
                there = slice(BLOCK * i, BLOCK * (i + 1))
                value_grad = value_grad + dot(grad_t[:, there], probs[i][h, :, cols])
                key_grad = key_grad + dot(query_t[:, there], scores_grad[i][:, cols])
            pair = jnp.concatenate([key_grad, value_grad], axis=0).astype(BF16).T
            filler = jnp.zeros((BLOCK, HD), BF16)
            plo[s, cols, first] = jnp.concatenate([dq[cols, :], pair, filler], axis=1)

    def head_weights(s, t):
        out = g_own if s == 0 else g_oth
        cols = rows_of(t * BLOCK, BLOCK, BLOCK)
        product = dot(plo[s, :, cols], n1[...], TN)
        out[rows_of(2 * hidden + t * BLOCK + HD, 3 * HD), :] = product[:3 * HD].astype(BF16)

    def back(t, _):
        for s in (1, 0):
            service_at(f"ab{s}", t, nh)
            head_back(s, t)
            service_at(f"gq{s}", t, nh)
            head_weights(s, t)
            ready_at(6, t, s)
        return 0

    lax.fori_loop(0, nh, back, 0)

    def norm1_part(here):
        total = None
        for s in range(2):
            for h in range(nh):
                t = plo[s, here, pl.ds(h * BLOCK, 3 * HD)]
                spot = (pl.ds(QVB + 8 * s, 1), pl.ds(h * BLOCK, 3 * HD))
                sm_a[spot] = sm_a[spot] + jnp.sum(t.astype(F32), axis=0, keepdims=True)
                weights = jnp.concatenate([wqkv[s, j, pl.ds(h * HD, HD), :] for j in range(3)], axis=0)
                product = dot(t, weights)
                total = product if total is None else total + product
        return total

    def norm1_theirs(m, _):
        service_at("n1", m, hblk)
        here = rows_of(theirs + m * BLOCK, BLOCK)
        mg[here, :] = norm1_part(here).astype(BF16)
        return 0

    norm1_copy = to_core(10, mg.at[rows_of(theirs, half)], r_attn)
    lax.fori_loop(0, hblk, norm1_theirs, 0)
    norm1_copy.start()

    def mlp_part(here, cols):
        return dot(act_t[0, :, here], wproj[0, :, cols], TN) + dot(act_t[1, :, here], wproj[1, :, cols], TN)

    def mlp_theirs(n, _):
        service_at("mlpa", n, width // BLOCK)
        cols = rows_of(n * BLOCK, BLOCK, BLOCK)
        send_a[:, cols] = mlp_part(rows_of(theirs, half, BLOCK), cols).astype(BF16)
        return 0

    def mlp_mine(n, _):
        service_at("mlpb", n, width // BLOCK)
        cols = rows_of(n * BLOCK, BLOCK, BLOCK)
        hid[:, cols] = hid[:, cols] + SCALE * (mlp_part(rows_of(mine, half, BLOCK), cols) + pb[cols].reshape(1, -1))
        return 0

    mlp_copy = to_core(6, send_a, r_n2)
    lax.fori_loop(0, width // BLOCK, mlp_theirs, 0)
    mlp_copy.start()

    norm1_copy.wait()
    sums = [jnp.zeros((1, width), F32) for _ in range(2)]
    for i in range(hblk):
        service(f"ln1b.{i}")
        here = pl.ds(i * BLOCK, BLOCK)
        grad = norm1_part(rows_of(mine + i * BLOCK, BLOCK)) + r_attn[here, :].astype(F32)
        normal, rate = centre(x_ref[here, :].astype(F32))
        n1_copy(i).wait_send()
        n1[rows_of(mine + i * BLOCK, BLOCK), :] = (hg[here, :] + norm_back(grad, line(g1), normal, rate)).astype(BF16)
        sums[0] = sums[0] + jnp.sum(grad * normal, axis=0, keepdims=True)
        sums[1] = sums[1] + jnp.sum(grad, axis=0, keepdims=True)
    sm_a[pl.ds(LN1G, 1), :] = sums[0]
    sm_a[pl.ds(LN1B, 1), :] = sums[1]
    input_result = pltpu.make_async_copy(n1.at[rows_of(mine, half)], input_grad, ks.at[len(ORDERS) + 1])
    input_result.start()
    small_copy(0).start()

    lax.fori_loop(0, width // BLOCK, mlp_mine, 0)
    mlp_copy.wait()
    service("out")
    for i in range(hblk):
        n2_copy(i).wait_send()
        here = pl.ds(i * BLOCK, BLOCK)
        there = rows_of(mine + i * BLOCK, BLOCK)
        n2[there, :] = (hid[here, :] + SCALE * r_n2[here, :].astype(F32)).astype(BF16)
    result = pltpu.make_async_copy(n2.at[rows_of(mine, half)], layer_out, ks.at[len(ORDERS)])
    result.start()

    service("end")
    for k in range(len(ORDERS)):
        for stage in range(len(stages[k])):
            for copy in grad_copies(k, stage):
                copy.wait_send()
        for i in range(3):
            gather_copy(k, i).wait_send()
    for j in range(8):
        for way in ("y", "x", "z1", "last"):
            weight_copy(j, way).wait_send()
    for copy in (copy_qvb, copy_fcb, mg_copy):
        copy.wait_send()
    for i in range(hblk):
        ag_copy(i).wait_send()
    result.wait()
    input_result.wait()


def shards(
    inputs, cotangent, ln1_gain, ln1_bias, w_qkv, qv_bias, w_out, out_bias, ln2_gain, ln2_bias,
    w_fc, fc_bias, w_proj, proj_bias, doc_lengths,
):
    half, width = inputs.shape
    rows = 2 * half
    shard = w_out.shape[0]
    nh = shard // HD
    heads = 2 * nh
    hidden = w_proj.shape[0]
    nblk = rows // BLOCK
    count = len(ORDERS)
    vmem = pl.BlockSpec(memory_space=pltpu.VMEM)
    hbm = pl.BlockSpec(memory_space=pl.ANY)
    smem = pl.BlockSpec(memory_space=pltpu.SMEM)

    def low(*shape):
        return pltpu.VMEM(shape, BF16)

    def full(*shape):
        return pltpu.VMEM(shape, F32)

    dma = pltpu.SemaphoreType.DMA
    square = jax.ShapeDtypeStruct((hidden, width), BF16)
    layer_out, input_grad, proj, fc, att, small = pl.pallas_call(
        block_kernel,
        out_shape=(
            jax.ShapeDtypeStruct((half, width), BF16),
            jax.ShapeDtypeStruct((half, width), BF16),
            square, square, square,
            jax.ShapeDtypeStruct((8, width), F32),
        ),
        in_specs=[vmem, vmem, vmem, vmem, hbm, vmem, hbm, vmem, vmem, vmem, hbm, vmem, hbm, vmem, smem],
        out_specs=(hbm, hbm, hbm, hbm, hbm, vmem),
        scratch_shapes=[
            low(2, 3, shard, width), low(2, shard, width), low(2, width, hidden), low(2, hidden, width),
            full(2, shard), full(hidden),
            low(rows, width), low(rows, width), low(rows, width), low(rows, width),
            *[low(heads, rows, HD) for _ in range(5)],
            *[low(heads, BLOCK, BLOCK * (i + 1)) for i in range(nblk)],
            *[low(BLOCK, BLOCK * (i + 1)) for i in range(nblk)],
            low(rows, HD), low(2, hidden, rows), low(2, rows, hidden), full(half, width), full(half, width),
            *[low(half, width) for _ in range(3)],
            low(count * BLOCK, width), low(count * BLOCK, width), low(count * BLOCK // 8 * 15, width),
            pltpu.VMEM((rows, 1), jnp.int32),
            full(16, width), full(16, width), full(3, 8, width), full(5, 8, width),
            dma((16,)), dma((16,)), dma((4, 10)), dma((4, 10)), dma((4,)),
            dma((count, 11)), dma((count, 11)), dma((count + 2,)),
        ],
        compiler_params=pltpu.CompilerParams(
            collective_id=0, has_side_effects=True, vmem_limit_bytes=66_500_000
        ),
        name="block",
    )(
        inputs, cotangent, ln1_gain, ln1_bias, w_qkv.transpose(0, 2, 1), qv_bias, w_out, out_bias,
        ln2_gain, ln2_bias, w_fc, fc_bias, w_proj, proj_bias, doc_lengths,
    )
    devices = lax.axis_size("dp")
    if devices > 8:
        groups = [[g * 8 + i for g in range(devices // 8)] for i in range(8)]
        proj, fc, att, small = lax.psum(
            (proj.astype(F32), fc.astype(F32), att.astype(F32), small), "dp", axis_index_groups=groups
        )
    heads_first = att.reshape(nh, 4, HD, width)
    out_grad = heads_first[:, 0].reshape(shard, width).astype(F32)
    qkv_grad = heads_first[:, 1:].transpose(1, 0, 2, 3).reshape(3, shard, width).astype(F32).transpose(0, 2, 1)
    by_head = small[QVB].reshape(nh, BLOCK)
    qv_grad = jnp.stack([by_head[:, :HD].reshape(shard), by_head[:, 2 * HD:3 * HD].reshape(shard)])
    return (
        layer_out, input_grad, small[LN1G], small[LN1B], qkv_grad, qv_grad, out_grad, small[OUTB],
        small[LN2G], small[LN2B], fc.astype(F32), small[FCB], proj.astype(F32), small[PROJB],
    )


def solution(mesh):
    tokens = P(("dp", "mp"), None)
    in_specs = (
        tokens, tokens, P(), P(), P(None, None, "mp"), P(None, "mp"), P("mp", None), P(), P(), P(),
        P(None, "mp"), P("mp"), P("mp", None), P(), P("dp", None),
    )
    out_specs = (
        tokens, tokens, P(), P(), P(None, None, "mp"), P(None, "mp"), P("mp", None), P(), P(), P(),
        P(None, "mp"), P("mp"), P("mp", None), P(),
    )
    return jax.shard_map(shards, mesh=mesh, in_specs=in_specs, out_specs=out_specs, check_vma=False)
```

time: 221 us -> 157 us (0.71)
  Pallas kernels: 195 us -> 144 us
  local copies, waits for them, and re-layouts: 21.5 us -> 7.08 us
    pallas_call x1, Pallas kernels: 195 us -> 144 us  [shards(): pl.pallas_call(block_kernel, out_shape=(jax.ShapeDtypeStruct((half, width...]
    broadcast_in_dim x7 -> x0, local copies, waits for them, and re-layouts: 8.87 us -> none  [the longest x1 1.27 us: shards(): ln1_gain[None]]
    slice x4 -> x2, local copies, waits for them, and re-layouts: 4.48 us -> 0.99 us  [the longest x1 0.98 us: shards(): out_grad = heads_first[:, 0].reshape(shard, width).astype(F32)]
    unnamed x9 -> x12, local copies, waits for them, and re-layouts: 4.96 us -> 2.89 us
where the time goes in v2:
time: 157 us; the launch traced here: 156 us
  Pallas kernels  144 us (92%)
  local copies, waits for them, and re-layouts  7.08 us (5%)
  other arithmetic  4.77 us (3%)
    pallas_call x1, Pallas kernels, shards(): pl.pallas_call(block_kernel, out_shape=(jax.ShapeDtypeStruct((half, width...  144 us

profile of v2, /device:TPU:0, one launch (start us, length us, event | category | flops | bytes accessed | tf_op | source)
XLA Modules:
  0.0 156.5 jit_solution(10666827301992248132)
XLA Ops:
  0.7 143.9 %block.1 = (bf16[512,768]{1,0:T(8,128)(2,1)}, bf16[512,768]{1,0:T(8,128)(2,1)}, bf16[768,768]{1,0:T(8,128)(2,1)}, bf16[768,768]{1,0:T(8,128)(2,1)}, bf16[768,768]{1,0:T(8,128)(2,1)}, /*index=5*/f32[8,768]{1,0:T(8,128)}) custom-call(bf16[512,768]{1,0:T(8,128)(2,1)} %x_ref.1, bf16[512,768]{1,0:T(8,128)(2,1)} %cot_ref.1, f32[768]{0:T(1024)} %g1.1, f32[768]{0:T(1024)} %b1.1, ...), custom_call_target="tpu_custom_call" | custom-call | tf_op jit(solution)/shard_map/block/pallas_call | solution.py:730
  144.6 0.0 copy-start.2
  144.6 1.7 %slice_reduce_fusion = (f32[768]{0:T(1024)}, f32[768]{0:T(1024)}, f32[768]{0:T(1024)}, f32[768]{0:T(1024)}, f32[768]{0:T(1024)}, /*index=5*/f32[768]{0:T(1024)S(1)}, f32[768]{0:T(1024)}, f32[768]{0:T(1024)}) fusion(f32[8,768]{1,0:T(8,128)} %get-tuple-element.22), kind=kLoop, calls=%fused_computation.2 | loop fusion | bytes 49152 | tf_op jit(solution)/shard_map/slice | solution.py:776
  146.3 0.1 stack_reshape.6
  146.4 0.1 stack_reshape.7
  146.5 0.6 pad_maximum_fusion
  147.1 1.0 slice.51
  148.1 0.9 bitcast_convert_fusion
  149.0 0.0 copy-done.2
  149.0 0.2 convert_bitcast_fusion
  149.1 0.0 copy-start.1
  149.1 1.3 copy.29
  150.5 0.5 copy-done.1
  150.9 0.0 copy-start
  150.9 1.6 %convert_element_type.23 = f32[768,768]{1,0:T(8,128)} convert(bf16[768,768]{1,0:T(8,128)(2,1)S(1)} %copy-done.1) | non-fusion elementwise | flops 589824 | bytes 3538944 | tf_op jit(solution)/shard_map/convert_element_type | solution.py:776
  152.5 0.1 copy-done
  152.6 0.0 copy-start.4
  152.6 1.6 %convert_element_type.24 = f32[768,768]{1,0:T(8,128)} convert(bf16[768,768]{1,0:T(8,128)(2,1)S(1)} %copy-done) | non-fusion elementwise | flops 589824 | bytes 3538944 | tf_op jit(solution)/shard_map/convert_element_type | solution.py:776
  154.2 0.0 copy-done.4
  154.2 0.0 copy-start.3
  154.2 0.9 copy.32
  155.1 0.5 copy-done.3
  155.6 0.9 copy.33
  (2 shorter events, 0.0 us)
Async XLA Ops:
  144.6 4.4 %copy-start.2 = (bf16[768,768]{1,0:T(8,128)(2,1)S(1)}, bf16[768,768]{1,0:T(8,128)(2,1)}, u32[]{:S(2)}) copy-start(bf16[768,768]{1,0:T(8,128)(2,1)} %get-tuple-element.23) | copy-start | bytes 3538948
  149.1 1.8 %copy-start.1 = (bf16[768,768]{1,0:T(8,128)(2,1)S(1)}, bf16[768,768]{1,0:T(8,128)(2,1)}, u32[]{:S(2)}) copy-start(bf16[768,768]{1,0:T(8,128)(2,1)} %get-tuple-element.24) | copy-start | bytes 3538948
  150.9 1.7 %copy-start = (bf16[768,768]{1,0:T(8,128)(2,1)S(1)}, bf16[768,768]{1,0:T(8,128)(2,1)}, u32[]{:S(2)}) copy-start(bf16[768,768]{1,0:T(8,128)(2,1)} %get-tuple-element.25) | copy-start | bytes 3538948
  152.6 1.6 %copy-start.4 = (bf16[512,768]{1,0:T(8,128)(2,1)S(1)}, bf16[512,768]{1,0:T(8,128)(2,1)}, u32[]{:S(2)}) copy-start(bf16[512,768]{1,0:T(8,128)(2,1)} %get-tuple-element.50) | copy-start | bytes 2359300
  154.2 1.4 copy-start.3

commit v3 on v2

--- a/solution.py
+++ b/solution.py
@@ -17,45 +17,52 @@
 TN = (((0,), (0,)), ((), ()))
 BLOCK = 256
 LN1G, LN1B, OUTB, LN2G, LN2B, PROJB, FCB, QVB = range(8)
-ORDERS = (
-    ("y", "x", "z2", "z1"),
-    ("z1", "y", "x", "z2"),
-    ("x", "y", "z1", "z2"),
-    ("z1", "y", "x", "z2"),
-    ("x", "y", "z1", "z2"),
-    ("z1", "y", "x", "z2"),
-    ("z1", "y", "x", "z2"),
-    ("x", "y", "z2", "z1"),
-    ("y", "x", "z1", "z2"),
+CHUNKS = (
+    (0, 0, 1, ("y", "x", "z1", "z2")),
+    (1, 0, 1, ("x", "z", "y")),
+    (2, 0, 1, ("z1", "y", "x", "z2")),
+    (3, 0, 1, ("z1", "y", "x", "z2")),
+    (4, 0, 1, ("x", "y", "z1", "z2")),
+    (5, 0, 1, ("y", "x", "z1", "z2")),
+    (6, 0, 1, ("x", "y", "z")),
+    (7, 0, 1, ("y", "z1", "x", "z2")),
+    (8, 0, 1, ("y", "x", "z")),
 )
-ROUTES = ("z1", "x", "z1", "x", "z1", "x", "z1", "x")
-SENDS = (0, 1, 2, 3, 4, 5, 6, 7)
+ROUTES = ("x", "x", "z1", "yx", "z1", "x", "z1", "y")
 SCHEDULE = {
-    "att0.0.0": (("w", 0, 0),),
-    "att0.0.1": (("w", 1, 0),),
+    "att0.1.0": (("w", 0, 0),),
+    "att0.1.1": (("w", 1, 0),),
     "att0.3.1": (("w", 2, 0),),
-    "att0.1.2": (("w", 0, 1),),
-    "needqkv": (("w", 1, 1), ("w", 2, 1), ("w", 3, 0), ("w", 4, 0), ("w", 5, 0),),
-    "att1.0.0": (("w", 3, 1), ("w", 6, 0),),
-    "att1.0.1": (("w", 4, 1),),
-    "att1.2.1": (("w", 7, 0),),
-    "att1.3.2": (("w", 5, 1),),
-    "ln2": (("w", 6, 1),),
-    "feed0.2": (("w", 7, 1),),
-    "mixb": (("g", 2, 0), ("g", 0, 0), ("g", 1, 0),),
-    "gq1.0": (("g", 4, 0), ("g", 3, 0),),
-    "gq0.0": (("g", 2, 1),),
-    "ab1.1": (("g", 0, 1), ("g", 5, 0),),
-    "gq0.1": (("g", 1, 1),),
-    "ab0.2": (("g", 2, 2), ("g", 4, 1),),
-    "mlpa.0": (("g", 6, 0), ("g", 3, 1),),
-    "mlpa.1": (("g", 1, 2),),
-    "ln1b.0": (("g", 0, 2),),
-    "ln1b.1": (("g", 2, 3), ("g", 5, 1), ("g", 7, 0), ("g", 4, 2),),
-    "mlpb.0": (("g", 3, 2), ("g", 1, 3), ("g", 0, 3),),
-    "mlpb.2": (("s", 0),),
-    "out": (("g", 5, 2),),
-    "end": (("g", 2, 4), ("g", 4, 3), ("g", 8, 0), ("g", 0, 4), ("g", 3, 3), ("g", 2, 5), ("g", 1, 4), ("g", 6, 1), ("g", 5, 3), ("g", 8, 1), ("g", 4, 4), ("g", 7, 1), ("s", 1), ("g", 2, 6), ("g", 8, 2), ("g", 0, 5), ("g", 1, 5), ("g", 4, 5), ("g", 3, 4), ("g", 6, 2), ("s", 2), ("g", 5, 4), ("g", 0, 6), ("g", 7, 2), ("g", 1, 6), ("g", 8, 3), ("s", 3), ("g", 4, 6), ("g", 7, 3), ("g", 6, 3), ("g", 3, 5), ("g", 8, 4), ("g", 7, 4), ("g", 5, 5), ("s", 4), ("g", 6, 4), ("g", 3, 6), ("g", 8, 5), ("g", 6, 5), ("g", 7, 5), ("g", 5, 6), ("g", 8, 6), ("g", 6, 6), ("g", 7, 6),),
+    "att0.3.2": (("w", 0, 1),),
+    "needqkv": (("w", 1, 1), ("w", 2, 1), ("w", 3, 0), ("w", 4, 0),),
+    "qkv1b": (("w", 5, 0),),
+    "att1.2.0": (("w", 6, 0),),
+    "att1.2.1": (("w", 4, 1),),
+    "att1.2.2": (("w", 5, 1),),
+    "feed0.0": (("w", 6, 1),),
+    "gfc0.0": (("g", 1, 0),),
+    "ln2b": (("g", 2, 0), ("g", 0, 0),),
+    "gq1.0": (("g", 4, 0),),
+    "gq0.0": (("g", 5, 0),),
+    "gq1.1": (("g", 0, 1), ("g", 1, 1),),
+    "ab0.1": (("g", 2, 1),),
+    "gq0.1": (("g", 3, 0),),
+    "gq1.2": (("g", 4, 1), ("g", 0, 2),),
+    "ab0.2": (("g", 1, 2),),
+    "gq0.2": (("g", 5, 1),),
+    "mlpa.0": (("g", 4, 2),),
+    "mlpa.2": (("g", 6, 0), ("g", 0, 3),),
+    "ln1b.1": (("g", 2, 2), ("g", 7, 0), ("g", 1, 3),),
+    "mlpb.0": (("g", 5, 2),),
+    "mlpb.2": (("g", 4, 3), ("g", 3, 1), ("s", 0),),
+    "out": (("g", 0, 4),),
+    "end": (
+        ("g", 2, 3), ("g", 1, 4), ("g", 7, 1), ("g", 3, 2), ("g", 5, 3), ("g", 4, 4), ("g", 8, 0), ("g", 0, 5),
+        ("g", 7, 2), ("g", 2, 4), ("g", 3, 3), ("g", 6, 1), ("s", 1), ("g", 5, 4), ("g", 4, 5), ("g", 8, 1),
+        ("g", 7, 3), ("g", 3, 4), ("g", 0, 6), ("g", 2, 5), ("s", 2), ("g", 5, 5), ("g", 6, 2), ("g", 4, 6),
+        ("g", 8, 2), ("g", 3, 5), ("g", 7, 4), ("g", 2, 6), ("s", 3), ("g", 5, 6), ("g", 7, 5), ("g", 6, 3),
+        ("g", 8, 3), ("g", 3, 6), ("g", 6, 4), ("s", 4), ("g", 8, 4), ("g", 7, 6),
+    ),
 }
 
 
@@ -85,14 +92,14 @@
 
 
 def block_kernel(
-    x_ref, cot_ref, g1, b1, wqkv_hbm, qvb, wout_hbm, ob, g2, b2, wfc_hbm, fcb, wproj_hbm, pb, docs,
+    x_hbm, cot_hbm, g1, b1, wqkv_hbm, qvb, wout_hbm, ob, g2, b2, wfc_hbm, fcb, wproj_hbm, pb, docs,
     layer_out, input_grad, f_proj, f_fc, f_att, small_out,
-    wqkv, wout, wfc, wproj, qvb_o, fcb_o, n1, n2, mg, ag, qh, kh, vh, mxh, mgh, p0, p1, p2, p3,
+    x_ref, cot_ref, wqkv, wout, wfc, wproj, qvb_o, fcb_o, n1, n2, mg, qh, kh, vh, mxh, mgh, p0, p1, p2, p3,
     s0, s1, s2, s3, dq, act_t, plo, hid, hg, send_a, r_attn, r_n2,
-    g_own, g_oth, r_buf, lo, sm_a, sm_b, sm_c, sm_r,
+    g_own, g_oth, r_buf, lo, scales, sm_a, sm_b, sm_c, sm_r,
     cs, cr, ws, wr, ls, gs, gr, ks,
 ):
-    half, width = x_ref.shape
+    half, width = x_hbm.shape
     rows = 2 * half
     shard = wout_hbm.shape[0]
     nh = shard // HD
@@ -107,13 +114,16 @@
         "z1": lax.rem(lax.div(dp, 2), 2),
         "z2": lax.rem(lax.div(dp, 4), 2),
     }
+    zi = bits["z1"] + 2 * bits["z2"]
     targets = {
         "core": (dp, mp + 1 - 2 * core),
         "y": (dp, mp + 2 - 4 * y),
         "x": (dp + 1 - 2 * bits["x"], mp),
         "z1": (dp + 2 - 4 * bits["z1"], mp),
         "z2": (dp + 4 - 8 * bits["z2"], mp),
+        "z3": (dp + 6 - 4 * zi, mp),
     }
+    zs = {"z1": zi + 1 - 2 * bits["z1"], "z2": zi + 2 - 4 * bits["z2"], "z3": 3 - zi}
     mine, theirs = core * half, (1 - core) * half
     probs, scores_grad = (p0, p1, p2, p3), (s0, s1, s2, s3)
 
@@ -128,18 +138,21 @@
     barrier = pltpu.get_barrier_semaphore()
     for target in targets.values():
         pl.semaphore_signal(barrier, inc=1, device_id=target, device_id_type=MESH)
+    x_copy = pltpu.make_async_copy(x_hbm, x_ref, ls.at[4])
+    cot_copy = pltpu.make_async_copy(cot_hbm, cot_ref, ls.at[5])
+    x_copy.start()
     pl.semaphore_wait(barrier, len(targets))
 
     group = bits["x"] + 2 * bits["z1"]
     beside = {"x": group + 1 - 2 * bits["x"], "z1": group + 2 - 4 * bits["z1"]}
 
-    def slot_piece(ref, lead, j, index):
+    def slot_piece(ref, lead, j, index, count=1):
         if j < 3:
-            return ref.at[(*lead, j, rows_of(index * (shard // 4), shard // 4))]
+            return ref.at[(*lead, j, rows_of(index * (shard // 4), count * (shard // 4)))]
         if j == 3:
-            return ref.at[(*lead, rows_of(index * (shard // 4), shard // 4))]
+            return ref.at[(*lead, rows_of(index * (shard // 4), count * (shard // 4)))]
         size = width // 8
-        return ref.at[(*lead, rows_of((j % 2) * 4 * size + index * size, size))]
+        return ref.at[(*lead, rows_of((j % 2) * 4 * size + index * size, count * size))]
 
     def slot_refs(j):
         if j < 3:
@@ -148,15 +161,24 @@
             return wout_hbm, wout
         return (wfc_hbm, wfc) if j < 6 else (wproj_hbm, wproj)
 
+    def ways_of(j):
+        route = ROUTES[j]
+        return ("y",) if route == "y" else ("y", "last") if route[0] == "y" else ("y", "x", "z1", "last")
+
     def weight_copy(j, way):
         hbm, vmem = slot_refs(j)
+        route = ROUTES[j]
+        axis = way if way != "last" else route[1:] if route[0] == "y" else route
+        index, count = group, 1
+        if route == "y":
+            index, count = 0, 4
+        elif route[0] == "y":
+            index, count = 2 * bits[route[1:]], 2
+        elif way == "last":
+            index = beside["x" if axis == "z1" else "z1"]
+        dst = slot_piece(vmem, (1,), j, index, count)
+        src = slot_piece(hbm, (), j, index, count) if way == "y" else dst
         number = ("y", "x", "z1", "last").index(way)
-        if way == "y":
-            src, dst, axis = slot_piece(hbm, (), j, group), slot_piece(vmem, (1,), j, group), "y"
-        else:
-            axis = ROUTES[j] if way == "last" else way
-            index = group if way != "last" else beside["x" if axis == "z1" else "z1"]
-            src = dst = slot_piece(vmem, (1,), j, index)
         return remote(src, dst, ws.at[number, j], wr.at[number, j], axis)
 
     def weight_own(i):
@@ -170,8 +192,10 @@
     def weight_step(j, hop):
         if hop == 0:
             weight_copy(j, "y").wait_recv()
-            weight_copy(j, "x").start()
-            weight_copy(j, "z1").start()
+            arrived.add((j, "y"))
+            for way in ways_of(j)[1:]:
+                if way != "last" or ROUTES[j][0] == "y":
+                    weight_copy(j, way).start()
         else:
             way = "x" if ROUTES[j] == "z1" else "z1"
             weight_copy(j, way).wait_recv()
@@ -180,65 +204,72 @@
 
     def need(slots):
         for j in slots:
-            for way in ("x", "z1", "last"):
+            for way in ways_of(j):
                 if (j, way) not in arrived:
                     weight_copy(j, way).wait_recv()
 
-    each = BLOCK + BLOCK // 2 + BLOCK // 4 + BLOCK // 8
-    stages = []
-    for k, order in enumerate(ORDERS):
-        offset, size, at, whole, plan = k * BLOCK, BLOCK, k * each, True, []
+    plans, at = [], 0
+    for unit, part, parts, order in CHUNKS:
+        size = BLOCK // parts
+        offset, whole, plan = unit * BLOCK + part * size, True, []
         for axis in order:
+            copies = []
             if axis == "y":
-                plan.append((axis, offset, offset, size, at, False))
-                at, whole = at + size, False
+                whole = False
+                copies.append(("y", True, offset, at))
+                at += size
             else:
-                size //= 2
-                keep, give = offset + bits[axis] * size, offset + (1 - bits[axis]) * size
-                plan.append((axis, keep, give, size, at, whole))
-                at, offset = at + size * (2 if whole else 1), keep
-        stages.append(plan)
-
-    def grad_copies(k, stage, only=(True, True)):
-        axis, _, give, size, at, whole = stages[k][stage]
-        parts = []
-        if axis != "y":
-            parts.append((g_own, 0))
-        if axis == "y" or whole:
-            parts.append((g_oth, len(parts)))
-        parts = [part for part in parts if only[part[0] is g_oth]]
+                size //= 4 if axis == "z" else 2
+                place = zi if axis == "z" else bits[axis]
+                for other in (False, True)[:2 if whole else 1]:
+                    for way in ("z1", "z2", "z3") if axis == "z" else (axis,):
+                        give = zs[way] if axis == "z" else 1 - place
+                        copies.append((way, other, offset + give * size, at))
+                        at += size
+                offset = offset + place * size
+            plan.append((axis, offset, size, copies))
+        plans.append(plan)
+
+    def grad_copy(k, stage, i):
+        _, _, size, copies = plans[k][stage]
+        way, other, start, there = copies[i]
+        number = sum(len(entry[3]) for entry in plans[k][:stage]) + i
+        return remote(
+            (g_oth if other else g_own).at[rows_of(start, size)], r_buf.at[rows_of(there, size)],
+            gs.at[k, number], gr.at[k, number], way,
+        )
+
+    results = (f_proj, f_fc, f_att)
+
+    def result_rows(k, start, size):
+        which = CHUNKS[k][0] // 3
+        return results[which].at[rows_of(start - which * 3 * BLOCK, size)]
+
+    def gather_plan(k):
+        return [entry for entry in reversed(plans[k]) if entry[0] != "y"]
+
+    def gather_copies(k, i):
+        axis, start, size, _ = gather_plan(k)[i]
+        src = g_own.at[rows_of(start, size)] if i == 0 else result_rows(k, start, size)
+        ways = ("z1", "z2", "z3") if axis == "z" else (axis,)
         return [
-            remote(
-                ref.at[rows_of(give, size)], r_buf.at[rows_of(at + i * size, size)],
-                gs.at[k, 2 * stage + i], gr.at[k, 2 * stage + i], axis,
-            )
-            for ref, i in parts
+            remote(src, result_rows(k, start, size), gs.at[k, 9 + 3 * i + n], gr.at[k, 9 + 3 * i + n], way)
+            for n, way in enumerate(ways)
         ]
 
-    results = (f_proj, f_fc, f_att)
-
-    def result_rows(k, start, size):
-        return results[k // 3].at[rows_of(start - (k // 3) * 3 * BLOCK, size)]
-
-    def gather_plan(k):
-        return [entry for entry in reversed(stages[k]) if entry[0] != "y"]
-
-    def gather_copy(k, i):
-        plan = gather_plan(k)
-        start, size = plan[i][1], plan[i][3]
-        src = g_own.at[rows_of(start, size)] if i == 0 else result_rows(k, start, size)
-        return remote(src, result_rows(k, start, size), gs.at[k, 8 + i], gr.at[k, 8 + i], plan[i][0])
-
     def keep_copy(k):
-        start, size = gather_plan(k)[0][1], gather_plan(k)[0][3]
+        _, start, size, _ = gather_plan(k)[0]
         return pltpu.make_async_copy(g_own.at[rows_of(start, size)], result_rows(k, start, size), ks.at[k])
 
-    def add(ref, start, size, at):
+    def add(ref, start, size, sources):
         step = min(size, BLOCK // 4)
 
         def body(m, _):
-            here, there = rows_of(start + m * step, step), rows_of(at + m * step, step)
-            ref[here, :] = (ref[here, :].astype(F32) + r_buf[there, :].astype(F32)).astype(BF16)
+            here = rows_of(start + m * step, step)
+            total = ref[here, :]
+            for there in sources:
+                total = total + r_buf[rows_of(there + m * step, step), :]
+            ref[here, :] = total
             return 0
 
         if size == step:
@@ -247,35 +278,44 @@
             lax.fori_loop(0, size // step, body, 0)
 
     def grad_step(k, stage):
-        if stage < len(stages[k]):
-            axis, keep, _, size, at, whole = stages[k][stage]
-            for copy in grad_copies(k, stage):
-                copy.wait_recv()
-            add(g_own, keep, size, at)
-            if whole:
-                add(g_oth, keep, size, at + size)
-            if stage + 1 < len(stages[k]):
-                for copy in grad_copies(k, stage + 1):
-                    copy.start()
+        if stage < len(plans[k]):
+            axis, keep, size, copies = plans[k][stage]
+            for i in range(len(copies)):
+                grad_copy(k, stage, i).wait_recv()
+            if axis == "y":
+                add(g_own, keep, size, [copies[0][3]])
+            else:
+                for ref, other in ((g_own, False), (g_oth, True)):
+                    sources = [copy[3] for copy in copies if copy[1] == other]
+                    if sources:
+                        add(ref, keep, size, sources)
+            if stage + 1 < len(plans[k]):
+                for i in range(len(plans[k][stage + 1][3])):
+                    grad_copy(k, stage + 1, i).start()
             else:
                 keep_copy(k).start()
-                gather_copy(k, 0).start()
+                for copy in gather_copies(k, 0):
+                    copy.start()
         else:
-            i = stage - len(stages[k])
-            gather_copy(k, i).wait_recv()
+            i = stage - len(plans[k])
+            for copy in gather_copies(k, i):
+                copy.wait_recv()
             if i == 0:
                 keep_copy(k).wait()
-            if i < 2:
-                gather_copy(k, i + 1).start()
-
-    def grad_ready(k, other):
-        for copy in grad_copies(k, 0, (not other, other)):
-            copy.start()
+            if i + 1 < len(gather_plan(k)):
+                for copy in gather_copies(k, i + 1):
+                    copy.start()
+
+    def unit_ready(unit, s):
+        for k, chunk in enumerate(CHUNKS):
+            if chunk[0] == unit:
+                for i, copy in enumerate(plans[k][0][3]):
+                    if copy[1] == (s == 1):
+                        grad_copy(k, 0, i).start()
 
     def ready_at(first, t, s):
         for i in range(3):
-            if s == 1 or ORDERS[first + i][0] != "y":
-                pl.when(t == i)(lambda i=i: grad_ready(first + i, s == 1))
+            pl.when(t == i)(lambda i=i: unit_ready(first + i, s))
 
     ways = ("core", "y", "x", "z1", "z2")
 
@@ -307,13 +347,15 @@
             if f"{point}.{i}" in SCHEDULE:
                 pl.when(t == i)(lambda i=i: service(f"{point}.{i}"))
 
-    weight_own(0).start()
     copy_qvb.start()
-    for j in SENDS:
+    for j in range(len(ROUTES)):
         weight_copy(j, "y").start()
     copy_fcb.start()
-    for i in range(1, 4):
+    for i in range(4):
         weight_own(i).start()
+    cot_copy.start()
+    scales[...] = jnp.zeros_like(scales)
+    x_copy.wait()
 
     def n1_copy(i):
         view = n1.at[rows_of(mine + i * BLOCK, BLOCK)]
@@ -357,20 +399,36 @@
     def attend(s):
         def head(t, _):
             h = s * nh + t
-            for i in range(nblk):
-                service_at(f"att{s}.{i}", t, nh)
-                seen = BLOCK * (i + 1)
-                here = pl.ds(BLOCK * i, BLOCK)
-                score = dot(qh[h, here, :], kh[h, pl.ds(0, seen), :], NT)
-                key = lax.broadcasted_iota(jnp.int32, (BLOCK, seen), 1)
-                query = lax.broadcasted_iota(jnp.int32, (BLOCK, seen), 0) + BLOCK * i
-                score = jnp.where((key >= lo[here, :]) & (key <= query), score, -1e30)
-                peak = jnp.max(score, axis=-1, keepdims=True)
-                exponent = jnp.exp(score - peak)
-                scale = 1.0 / jnp.sum(exponent, axis=-1, keepdims=True)
-                low = (exponent * scale).astype(BF16)
-                probs[i][h] = low
-                mxh[h, here, :] = dot(low, vh[h, pl.ds(0, seen), :]).astype(BF16)
+            values_t = vh[h].T
+            for n in range(nblk):
+                i = nblk - 1 - n
+                service_at(f"att{s}.{n}", t, nh)
+                here, before, seen = pl.ds(BLOCK * i, BLOCK), pl.ds(0, BLOCK * i), BLOCK * i
+                first = lo[here, :]
+                key = lax.broadcasted_iota(jnp.int32, (BLOCK, BLOCK), 1) + seen
+                query = lax.broadcasted_iota(jnp.int32, (BLOCK, BLOCK), 0) + seen
+                near = dot(qh[h, here, :], kh[h, here, :], NT)
+                near = jnp.where((key >= first) & (key <= query), near, -1e30)
+                peak = jnp.max(near, axis=-1, keepdims=True)
+                if i:
+                    far = dot(qh[h, here, :], kh[h, before, :], NT)
+                    far = jnp.where(lax.broadcasted_iota(jnp.int32, (BLOCK, seen), 1) >= first, far, -1e30)
+                    peak = jnp.maximum(peak, jnp.max(far, axis=-1, keepdims=True))
+                near = jnp.exp(near - peak)
+                total = jnp.sum(near, axis=-1, keepdims=True)
+                near = near.astype(BF16)
+                probs[i][h, :, here] = near
+                mixed_t = dot(values_t[:, seen:seen + BLOCK], near, NT)
+                if i:
+                    far = jnp.exp(far - peak)
+                    total = total + jnp.sum(far, axis=-1, keepdims=True)
+                    far = far.astype(BF16)
+                    probs[i][h, :, before] = far
+                    mixed_t = mixed_t + dot(values_t[:, :seen], far, NT)
+                scale = 1.0 / total
+                mxh[h, here, :] = (mixed_t.T * scale).astype(BF16)
+                lane = lax.broadcasted_iota(jnp.int32, (BLOCK, scales.shape[1]), 1)
+                scales[here, :] = jnp.where(lane == h, scale, scales[here, :])
             return 0
 
         lax.fori_loop(0, nh, head, 0)
@@ -387,6 +445,7 @@
 
     service("mg")
     mg_copy = to_core(2, mg.at[rows_of(mine, half)], mg.at[rows_of(mine, half)])
+    cot_copy.wait()
     total = jnp.zeros((1, width), F32)
     for i in range(hblk):
         values = cot_ref[pl.ds(i * BLOCK, BLOCK), :].astype(F32)
@@ -446,8 +505,12 @@
         n2[rows_of(mine + i * BLOCK, BLOCK), :] = (normal * line(g2) + line(b2)).astype(BF16)
         n2_copy(i).start()
 
+    def others_here():
+        for i in range(hblk):
+            n2_copy(i).wait_recv()
+        mg_copy.wait_recv()
+
     def feed(s):
-        bias = line(fcb if s == 0 else fcb_o)
         a, b = math.sqrt(2 / math.pi), math.sqrt(2 / math.pi) * 0.044715
         out = g_own if s == 0 else g_oth
 
@@ -455,8 +518,10 @@
             service_at(f"feed{s}", f, hidden // BLOCK)
             cols = rows_of(f * BLOCK, BLOCK, BLOCK)
             total = jnp.zeros((1, BLOCK), F32)
-            for m in range(2):
-                here = pl.ds(half * m, half)
+            for m, start in enumerate((mine, theirs)):
+                here = rows_of(start, half, half)
+                if m == 1 and s == 0:
+                    pl.when(f == 0)(others_here)
                 u = dot(n2[here, :], wfc[s, :, cols]) + (fcb if s == 0 else fcb_o)[cols].reshape(1, -1)
                 up = dot(mg[here, :], wproj[s, cols, :], NT)
                 square = u * u
@@ -486,17 +551,14 @@
         lax.fori_loop(0, width // BLOCK, tile, 0)
 
     service("ln2")
-    for i in range(hblk):
-        n2_copy(i).wait_recv()
-    mg_copy.wait_recv()
     weight_own(2).wait()
     weight_own(3).wait()
     feed(0)
-    grad_fc(0)
     service("needfp")
     copy_fcb.wait_recv()
     need(range(4, 8))
     feed(1)
+    grad_fc(1)
 
     def norm2_part(here, cols):
         return dot(plo[0, here, :], wfc[0, cols, :], NT) + dot(plo[1, here, :], wfc[1, cols, :], NT)
@@ -517,12 +579,14 @@
     norm2_copy.start()
     service("n2b")
     lax.fori_loop(0, width // BLOCK, norm2_mine, 0)
-    grad_fc(1)
+    grad_fc(0)
     service("ln2b")
     norm2_copy.wait()
 
+    mg_copy.wait_send()
+
     def ag_copy(i):
-        view = ag.at[rows_of(mine + i * BLOCK, BLOCK)]
+        view = mg.at[rows_of(mine + i * BLOCK, BLOCK)]
         return to_core(8 + i, view, view)
 
     sums = [jnp.zeros((1, width), F32) for _ in range(3)]
@@ -532,7 +596,7 @@
         normal, rate = centre(hid[here, :])
         state_grad = cot_ref[here, :].astype(F32) + norm_back(grad, line(g2), normal, rate)
         hg[here, :] = state_grad
-        ag[rows_of(mine + i * BLOCK, BLOCK), :] = (SCALE * state_grad).astype(BF16)
+        mg[rows_of(mine + i * BLOCK, BLOCK), :] = (SCALE * state_grad).astype(BF16)
         ag_copy(i).start()
         for j, value in enumerate((grad * normal, grad, SCALE * state_grad)):
             sums[j] = sums[j] + jnp.sum(value, axis=0, keepdims=True)
@@ -543,11 +607,12 @@
     def mixed_grad(start):
         def body(m, _):
             here = rows_of(start + m * BLOCK, BLOCK)
-            tokens = ag[here, :]
+            tokens = mg[here, :]
             for s in range(2):
-                t = dot(tokens, wout[s], NT).astype(BF16)
+                t = dot(tokens, wout[s], NT)
                 for h in range(nh):
-                    mgh[s * nh + h, here, :] = t[:, h * HD:(h + 1) * HD]
+                    scale = scales[here, s * nh + h:s * nh + h + 1]
+                    mgh[s * nh + h, here, :] = (t[:, h * HD:(h + 1) * HD] * scale).astype(BF16)
             return 0
 
         lax.fori_loop(0, hblk, body, 0)
@@ -564,7 +629,7 @@
 
         def tile(n, _):
             cols = rows_of(n * BLOCK, BLOCK, BLOCK)
-            product = dot(mixed_of(s, slice(None)), ag[:, cols], TN).astype(BF16)
+            product = dot(mixed_of(s, slice(None)), mg[:, cols], TN).astype(BF16)
             for h in range(nh):
                 out[pl.ds(2 * hidden + h * BLOCK, HD), cols] = product[h * HD:(h + 1) * HD]
             return 0
@@ -670,7 +735,7 @@
         sums[1] = sums[1] + jnp.sum(grad, axis=0, keepdims=True)
     sm_a[pl.ds(LN1G, 1), :] = sums[0]
     sm_a[pl.ds(LN1B, 1), :] = sums[1]
-    input_result = pltpu.make_async_copy(n1.at[rows_of(mine, half)], input_grad, ks.at[len(ORDERS) + 1])
+    input_result = pltpu.make_async_copy(n1.at[rows_of(mine, half)], input_grad, ks.at[len(CHUNKS) + 1])
     input_result.start()
     small_copy(0).start()
 
@@ -682,25 +747,80 @@
         here = pl.ds(i * BLOCK, BLOCK)
         there = rows_of(mine + i * BLOCK, BLOCK)
         n2[there, :] = (hid[here, :] + SCALE * r_n2[here, :].astype(F32)).astype(BF16)
-    result = pltpu.make_async_copy(n2.at[rows_of(mine, half)], layer_out, ks.at[len(ORDERS)])
+    result = pltpu.make_async_copy(n2.at[rows_of(mine, half)], layer_out, ks.at[len(CHUNKS)])
     result.start()
 
     service("end")
-    for k in range(len(ORDERS)):
-        for stage in range(len(stages[k])):
-            for copy in grad_copies(k, stage):
+    for k in range(len(CHUNKS)):
+        for stage in range(len(plans[k])):
+            for i in range(len(plans[k][stage][3])):
+                grad_copy(k, stage, i).wait_send()
+        for i in range(len(gather_plan(k))):
+            for copy in gather_copies(k, i):
                 copy.wait_send()
-        for i in range(3):
-            gather_copy(k, i).wait_send()
-    for j in range(8):
-        for way in ("y", "x", "z1", "last"):
+    for j in range(len(ROUTES)):
+        for way in ways_of(j):
             weight_copy(j, way).wait_send()
-    for copy in (copy_qvb, copy_fcb, mg_copy):
+    for copy in (copy_qvb, copy_fcb):
         copy.wait_send()
     for i in range(hblk):
         ag_copy(i).wait_send()
     result.wait()
     input_result.wait()
+
+
+def finish(
+    proj_in, fc_in, att_in, layer_in, grad_in, small,
+    proj_out, fc_out, out_out, qkv_out, layer_out, grad_out, ln1g, ln1b, outb, ln2g, ln2b, projb, fcb, qvb,
+    proj_low, fc_low, att_low, layer_low, grad_low, proj_full, fc_full, out_full, qkv_full, sems,
+):
+    nh = out_out.shape[0] // HD
+    loads = [
+        pltpu.make_async_copy(src, dst, sems.at[i])
+        for i, (src, dst) in enumerate(
+            (
+                (proj_in, proj_low), (fc_in, fc_low), (att_in, att_low), (layer_in, layer_low), (grad_in, grad_low),
+            )
+        )
+    ]
+    stores = [
+        pltpu.make_async_copy(src, dst, sems.at[5 + i])
+        for i, (src, dst) in enumerate(
+            (
+                (proj_full, proj_out), (fc_full, fc_out), (out_full, out_out), (qkv_full, qkv_out),
+                (layer_low, layer_out), (grad_low, grad_out),
+            )
+        )
+    ]
+    for copy in loads:
+        copy.start()
+    for row, ref in ((LN1G, ln1g), (LN1B, ln1b), (OUTB, outb), (LN2G, ln2g), (LN2B, ln2b), (PROJB, projb), (FCB, fcb)):
+        ref[...] = small[row, :]
+    for i in range(2):
+        cols = [slice(h * BLOCK + 2 * i * HD, h * BLOCK + (2 * i + 1) * HD) for h in range(nh)]
+        qvb[pl.ds(i, 1), :] = jnp.concatenate([small[pl.ds(QVB, 1), c] for c in cols], axis=1)
+    for i, (low, wide) in enumerate(((proj_low, proj_full), (fc_low, fc_full))):
+        loads[i].wait()
+
+        def body(m, _):
+            here = rows_of(m * BLOCK, BLOCK)
+            wide[here, :] = low[here, :].astype(F32)
+            return 0
+
+        lax.fori_loop(0, wide.shape[0] // BLOCK, body, 0)
+        stores[i].start()
+    for i in (3, 4):
+        loads[i].wait()
+        stores[i + 1].start()
+    loads[2].wait()
+    for h in range(nh):
+        out_full[pl.ds(h * HD, HD), :] = att_low[pl.ds(h * BLOCK, HD), :].astype(F32)
+        for j in range(3):
+            qkv_full[j, pl.ds(h * HD, HD), :] = att_low[pl.ds(h * BLOCK + (j + 1) * HD, HD), :].astype(F32)
+    stores[2].start()
+    stores[3].start()
+    for copy in stores:
+        copy.wait()
 
 
 def shards(
@@ -714,7 +834,8 @@
     heads = 2 * nh
     hidden = w_proj.shape[0]
     nblk = rows // BLOCK
-    count = len(ORDERS)
+    count = len(CHUNKS)
+    total = 2 * hidden + 4 * shard
     vmem = pl.BlockSpec(memory_space=pltpu.VMEM)
     hbm = pl.BlockSpec(memory_space=pl.ANY)
     smem = pl.BlockSpec(memory_space=pltpu.SMEM)
@@ -735,25 +856,25 @@
             square, square, square,
             jax.ShapeDtypeStruct((8, width), F32),
         ),
-        in_specs=[vmem, vmem, vmem, vmem, hbm, vmem, hbm, vmem, vmem, vmem, hbm, vmem, hbm, vmem, smem],
+        in_specs=[hbm, hbm, vmem, vmem, hbm, vmem, hbm, vmem, vmem, vmem, hbm, vmem, hbm, vmem, smem],
         out_specs=(hbm, hbm, hbm, hbm, hbm, vmem),
         scratch_shapes=[
-            low(2, 3, shard, width), low(2, shard, width), low(2, width, hidden), low(2, hidden, width),
+            low(half, width), low(half, width), low(2, 3, shard, width), low(2, shard, width), low(2, width, hidden), low(2, hidden, width),
             full(2, shard), full(hidden),
-            low(rows, width), low(rows, width), low(rows, width), low(rows, width),
+            low(rows, width), low(rows, width), low(rows, width),
             *[low(heads, rows, HD) for _ in range(5)],
             *[low(heads, BLOCK, BLOCK * (i + 1)) for i in range(nblk)],
             *[low(BLOCK, BLOCK * (i + 1)) for i in range(nblk)],
             low(rows, HD), low(2, hidden, rows), low(2, rows, hidden), full(half, width), full(half, width),
             *[low(half, width) for _ in range(3)],
-            low(count * BLOCK, width), low(count * BLOCK, width), low(count * BLOCK // 8 * 15, width),
-            pltpu.VMEM((rows, 1), jnp.int32),
+            low(total, width), low(total, width), low(total // 8 * 15, width),
+            pltpu.VMEM((rows, 1), jnp.int32), full(rows, 128),
             full(16, width), full(16, width), full(3, 8, width), full(5, 8, width),
-            dma((16,)), dma((16,)), dma((4, 10)), dma((4, 10)), dma((4,)),
-            dma((count, 11)), dma((count, 11)), dma((count + 2,)),
+            dma((16,)), dma((16,)), dma((4, 10)), dma((4, 10)), dma((6,)),
+            dma((count, 18)), dma((count, 18)), dma((count + 2,)),
         ],
         compiler_params=pltpu.CompilerParams(
-            collective_id=0, has_side_effects=True, vmem_limit_bytes=66_500_000
+            collective_id=0, has_side_effects=True, vmem_limit_bytes=66_000_000
         ),
         name="block",
     )(
@@ -766,14 +887,30 @@
         proj, fc, att, small = lax.psum(
             (proj.astype(F32), fc.astype(F32), att.astype(F32), small), "dp", axis_index_groups=groups
         )
-    heads_first = att.reshape(nh, 4, HD, width)
-    out_grad = heads_first[:, 0].reshape(shard, width).astype(F32)
-    qkv_grad = heads_first[:, 1:].transpose(1, 0, 2, 3).reshape(3, shard, width).astype(F32).transpose(0, 2, 1)
-    by_head = small[QVB].reshape(nh, BLOCK)
-    qv_grad = jnp.stack([by_head[:, :HD].reshape(shard), by_head[:, 2 * HD:3 * HD].reshape(shard)])
+    def vector(length):
+        return jax.ShapeDtypeStruct((length,), F32)
+
+    outs = pl.pallas_call(
+        finish,
+        out_shape=(
+            jax.ShapeDtypeStruct((hidden, width), F32), jax.ShapeDtypeStruct((width, hidden), F32),
+            jax.ShapeDtypeStruct((shard, width), F32), jax.ShapeDtypeStruct((3, shard, width), F32),
+            jax.ShapeDtypeStruct((half, width), BF16), jax.ShapeDtypeStruct((half, width), BF16),
+            *[vector(width) for _ in range(6)], vector(hidden), jax.ShapeDtypeStruct((2, shard), F32),
+        ),
+        in_specs=[hbm] * 5 + [vmem],
+        out_specs=(hbm,) * 6 + (vmem,) * 8,
+        scratch_shapes=[
+            *[pltpu.VMEM(ref.shape, ref.dtype) for ref in (proj, fc, att, layer_out, input_grad)],
+            full(hidden, width), full(width, hidden), full(shard, width), full(3, shard, width),
+            dma((11,)),
+        ],
+        compiler_params=pltpu.CompilerParams(vmem_limit_bytes=60 << 20),
+        name="finish",
+    )(proj, fc, att, layer_out, input_grad, small)
+    proj, fc, out, qkv, layer_out, input_grad, ln1g, ln1b, outb, ln2g, ln2b, projb, fcb, qvb = outs
     return (
-        layer_out, input_grad, small[LN1G], small[LN1B], qkv_grad, qv_grad, out_grad, small[OUTB],
-        small[LN2G], small[LN2B], fc.astype(F32), small[FCB], proj.astype(F32), small[PROJB],
+        layer_out, input_grad, ln1g, ln1b, qkv.transpose(0, 2, 1), qvb, out, outb, ln2g, ln2b, fc, fcb, proj, projb,
     )
 
 

time: 157 us -> 145 us (0.924)
  local copies, waits for them, and re-layouts: 7.08 us -> 0 us
  other arithmetic: 4.77 us -> 0 us
    pallas_call x0 -> x1, Pallas kernels: none -> 6.29 us  [shards(): pl.pallas_call(finish, out_shape=(jax.ShapeDtypeStruct((hidden, width), F...]
    pallas_call x1, Pallas kernels: 144 us -> 138 us  [shards(): pl.pallas_call(block_kernel, out_shape=(jax.ShapeDtypeStruct((half, width...]
    convert_element_type x3 -> x0, other arithmetic: 4.03 us -> none  [the longest x1 1.58 us: shards(): fc.astype(F32)]
    unnamed x12 -> x0, local copies, waits for them, and re-layouts: 2.89 us -> none
    slice x3 -> x0, local copies, waits for them, and re-layouts: 2.7 us -> none  [the longest x1 1.71 us: shards(): small[PROJB]]
where the time goes in v3:
time: 145 us
  Pallas kernels  144 us (99%)
    pallas_call x1, Pallas kernels, shards(): pl.pallas_call(block_kernel, out_shape=(jax.ShapeDtypeStruct((half, width...  138 us
    pallas_call x1, Pallas kernels, shards(): pl.pallas_call(finish, out_shape=(jax.ShapeDtypeStruct((hidden, width), F...  6.29 us

profile of v3, /device:TPU:0, one launch (start us, length us, event | category | flops | bytes accessed | tf_op | source)
XLA Modules:
  0.0 145.1 jit_solution(13766633811154664168)
XLA Ops:
  0.7 137.9 %block.1 = (bf16[512,768]{1,0:T(8,128)(2,1)}, bf16[512,768]{1,0:T(8,128)(2,1)}, bf16[768,768]{1,0:T(8,128)(2,1)}, bf16[768,768]{1,0:T(8,128)(2,1)}, bf16[768,768]{1,0:T(8,128)(2,1)}, /*index=5*/f32[8,768]{1,0:T(8,128)}) custom-call(bf16[512,768]{1,0:T(8,128)(2,1)} %x_hbm.1, bf16[512,768]{1,0:T(8,128)(2,1)} %cot_hbm.1, f32[768]{0:T(1024)} %g1.1, f32[768]{0:T(1024)} %b1.1, ...), custom_call_target="tpu_custom_call" | custom-call | tf_op jit(solution)/shard_map/block/pallas_call | solution.py:851
  138.6 6.3 %finish.1 = (f32[768,768]{1,0:T(8,128)}, f32[768,768]{1,0:T(8,128)}, f32[192,768]{1,0:T(8,128)}, f32[3,192,768]{2,1,0:T(8,128)}, bf16[512,768]{1,0:T(8,128)(2,1)...) custom-call(bf16[768,768]{1,0:T(8,128)(2,1)} %get-tuple-element.34.p, ...), custom_call_target="tpu_custom_call" | custom-call | tf_op jit(solution)/shard_map/finish/pallas_call | solution.py:893
